TPU v7x, 256 devices: a whole 4x4x8 slice. The times are simulated.
256 devices in a mesh: lon: 32 (over x_lo, z, core), lat: 8 (over x_hi, y).
Axes of the slice: x: 4 (x_hi: 2, x_lo: 2; x = x_hi * 2 + x_lo), y: 4, z: 8, core: 2. Of those that a mesh axis runs over, the one named last changes fastest.
Arguments:
- thermal_field: float32 [16, 512, 4096], P(None, 'lat', 'lon'), may hold values from -6 to 6
- elevation_now: float32 [512, 4096], P('lat', 'lon'), may hold values from -6 to 6
- elevation_prior: float32 [512, 4096], P('lat', 'lon'), may hold values from -6 to 6
- liquid_indicator: int32 [16, 512, 4096], P(None, 'lat', 'lon'), may hold values from 0 to 1, as said below
- seabed_depth: int32 [512, 4096], P('lat', 'lon'), may hold values from 0 to 16
- mixing_coefficients: float32 [16], replicated, may hold values from 0.03 to 0.2
- stencil_filter_matrices: bfloat16 [9, 128, 16], replicated, may hold values from -0.5 to 0.5
- inner_projection_matrix: bfloat16 [512, 128], replicated, may hold values from -0.5 to 0.5
- closing_projection_matrix: bfloat16 [16, 512], replicated, may hold values from -0.25 to 0.25
Outputs:
- corrected: float32 [16, 512, 4096], P(None, 'lat', 'lon')
- eta_out: float32 [512, 4096], P('lat', 'lon')
- eta_mid: float32 [512, 4096], P('lat', 'lon')
Inputs may be any that keep to these rules, and one draw needn't show every extreme that they name: `liquid_indicator`: 1 for water, 0 for land; whole continents of land span every level.
All inputs are finite; a program needn't handle non-finite values.
Results may differ from a plain program's by a relative error of at most 0.00033.
Values may be sent and summed in bfloat16 or wider, within the bound.
No kernel may reach another device: no remote copies, remote signals or barrier semaphores. Data moves between devices by JAX's collectives and lax.ppermute only.
A program may use at most 128 MiB of HBM per device.

v0:
```python
import jax
import jax.numpy as jnp
from jax import lax
from jax.experimental import pallas as pl
from jax.experimental.pallas import tpu as pltpu
from jax.sharding import PartitionSpec as P

SUB = 8
F32 = jnp.float32
BF16 = jnp.bfloat16
C0 = 0.7978845608028654
C1 = 0.044715 * C0
VM = pl.BlockSpec(memory_space=pltpu.VMEM)
SM = pl.BlockSpec(memory_space=pltpu.SMEM)
NT = (((1,), (1,)), ((), ()))


def iota(shape, axis):
    return lax.broadcasted_iota(jnp.int32, shape, axis)


def roll(x, shift, axis):
    size = x.shape[axis]
    shift = shift % size
    return x if shift == 0 else pltpu.roll(x, shift, axis)


def lanes_from(x, index):
    return jnp.take_along_axis(x, index, axis=1)


def gelu_twice(x):
    return x + x * jnp.tanh(x * (C0 + C1 * (x * x)))


def call(body, outs, scratch=(), specs=None, flops=0, moved=0, **given):
    return pl.pallas_call(
        body,
        out_shape=outs,
        in_specs=specs,
        out_specs=jax.tree.map(lambda _: VM, outs),
        scratch_shapes=list(scratch),
        compiler_params=pltpu.CompilerParams(vmem_limit_bytes=40 * 1024 * 1024),
        cost_estimate=pl.CostEstimate(flops=flops, bytes_accessed=moved, transcendentals=0),
        **given,
    )


def shape(*dims, dtype=F32):
    return jax.ShapeDtypeStruct(dims, dtype)


def inside(t_ref, l_ref, d_ref, now_ref, prior_ref, mix_ref,
           warm_ref, fk_ref, fc_ref, rt_ref, rf_ref, own_ref, pa_ref, pb_ref):
    lat = lax.axis_index("lat")
    dims = (64, 128)
    lane, row = iota(dims, 1), iota(dims, 0)
    depth = d_ref[...]
    column = jnp.zeros(dims, F32)
    forcing = jnp.zeros(dims, F32)
    rt = jnp.zeros(dims, F32)
    rf = jnp.zeros(dims, F32)

    def around(x):
        east = jnp.where(lane == 127, 0.0, roll(x, 127, 1))
        west = jnp.where(lane == 0, 0.0, roll(x, 1, 1))
        north = jnp.where(row == 63, 0.0, roll(x, 63, 0))
        south = jnp.where(row == 0, 0.0, roll(x, 1, 0))
        return (east + west) + (north + south)

    for k in range(16):
        t = t_ref[k]
        wet = jnp.where(k < depth, l_ref[k].astype(F32), 0.0)
        warm = t + (mix_ref[k] * wet) * (around(wet * t) - t * around(wet))
        feature = wet * warm
        warm_ref[k] = warm
        fk_ref[pl.ds(k, 64, stride=16), :] = feature
        column = column + wet
        forcing = forcing + feature
        rt = jnp.where(lane >> 1 == k, roll(t, 2 * k + 1, 1), rt)
        rt = jnp.where(lane >> 1 == 16 + k, roll(wet, 33 + 2 * k, 1), rt)
        rf = jnp.where(lane >> 3 == k, roll(feature, 8 * k + 4, 1), rf)
    forcing = 0.01 * forcing
    fc_ref[0] = forcing
    fc_ref[1] = column
    rt_ref[...] = rt
    rf_ref[...] = rf

    level = iota((16, 128), 0)

    def edge(r):
        wet = jnp.where(level < d_ref[r : r + 1, :], l_ref[:, r, :].astype(F32), 0.0)
        return t_ref[:, r, :], wet, fk_ref[16 * r : 16 * r + 16, :]

    def payload(r, first):
        t, wet, feature = edge(r)
        own = jnp.concatenate([t, wet], axis=0)
        rows = [x[first : first + 8] for x in (forcing, column, now_ref[...], prior_ref[...], rt)]
        return own, jnp.concatenate([own, feature] + rows, axis=0)

    own_low, low = payload(0, 0)
    own_high, high = payload(63, 56)
    own_ref[...] = jnp.concatenate([own_low, own_high], axis=0)
    even = lat % 2 == 0
    pa_ref[...] = jnp.where(even, high, low)
    pb_ref[...] = jnp.where(even, low, high)

    @pl.when(lat == 7)
    def _():
        small = (8, 128)
        back = 127 - iota(small, 1)
        swap = iota(small, 1) ^ 1
        for i in range(11):
            x = high[8 * i : 8 * i + 8]
            x = lanes_from(x, swap if i == 10 else back)
            if i >= 6:
                x = jnp.concatenate([x[j : j + 1] for j in range(7, -1, -1)], axis=0)
            pb_ref[8 * i : 8 * i + 8, :] = x


def between(pa_ref, pb_ref, own_ref, fk_ref, fc_ref, rt_ref, rf_ref, now_ref, prior_ref, mix_ref,
            e4_ref, fb_ref, dd_ref, rfx_ref, qa_ref, qb_ref):
    lat = lax.axis_index("lat")
    even = lat % 2 == 0
    pa, pb = pa_ref[...], pb_ref[...]
    high = jnp.where(even, pa, pb)
    low = jnp.where(lat == 0, 0.0, jnp.where(even, pb, pa))
    level, lane16 = iota((16, 128), 0), iota((16, 128), 1)
    mix = jnp.zeros((16, 128), F32)
    for k in range(16):
        mix = jnp.where(level == k, mix_ref[k], mix)

    def delta(halo, first):
        t, wet = own_ref[first : first + 16, :], own_ref[first + 16 : first + 32, :]
        return mix * (wet * halo[16:32]) * (halo[0:16] - t)

    d_low, d_high = delta(low, 0), delta(high, 32)
    dd_ref[0:16, :] = d_low
    dd_ref[16:32, :] = d_high
    f_out_low, f_low = low[32:48] - d_low, fk_ref[0:16, :] + d_low
    f_high, f_out_high = fk_ref[1008:1024, :] + d_high, high[32:48] - d_high
    fb_ref[...] = jnp.concatenate([f_out_low, f_low, f_high, f_out_high], axis=0)
    s_low = 0.01 * jnp.sum(d_low, axis=0, keepdims=True)
    s_high = 0.01 * jnp.sum(d_high, axis=0, keepdims=True)

    ext = (80, 128)
    lane, row = iota(ext, 1), iota(ext, 0)

    def extend(i, middle):
        first = 48 + 8 * i
        return jnp.concatenate([low[first : first + 8], middle, high[first : first + 8]], axis=0)

    forcing = extend(0, fc_ref[0])
    forcing = forcing + jnp.where(row == 8, s_low, 0.0) - jnp.where(row == 7, s_low, 0.0)
    forcing = forcing + jnp.where(row == 71, s_high, 0.0) - jnp.where(row == 72, s_high, 0.0)
    fields = [forcing, extend(1, fc_ref[1]), extend(2, now_ref[...]), extend(3, prior_ref[...])]
    mixed = extend(4, rt_ref[...])
    for i, field in enumerate(fields):
        e4_ref[i] = field
        mixed = jnp.where(lane >> 4 == 4 + i, roll(field, 72 + 16 * i, 1), mixed)

    def laid(f):
        x = pltpu.roll(f, 4, 1, stride=8, stride_axis=0)
        return jnp.sum(jnp.where(lane16 >> 3 == level, x, 0.0), axis=0, keepdims=True)

    zero = jnp.zeros((8, 128), F32)
    rf = jnp.concatenate([zero, rf_ref[...], zero], axis=0)
    for at, f in ((7, f_out_low), (8, f_low), (71, f_high), (72, f_out_high)):
        rf = jnp.where(row == at, laid(f), rf)
    rfx_ref[...] = rf

    small = iota((8, 128), 1)

    def columns(side):
        wide = 64 + 16 * ((small - 64) >> 3) + 8 * side + (small & 7)
        index = jnp.where(small < 32, 2 * small + side, jnp.where(small < 64, 0, wide))
        index_f = jnp.where((small >= 32) & (small < 48), 8 * (small - 32) + 3 + side, 0)
        parts = []
        for i in range(10):
            a = lanes_from(mixed[8 * i : 8 * i + 8], index)
            b = lanes_from(rf[8 * i : 8 * i + 8], index_f)
            parts.append(jnp.where((small >= 32) & (small < 48), b, a))
        return jnp.concatenate(parts, axis=0)

    first_core = lax.axis_index("lon") % 2 == 0
    q_east, q_west = columns(0), columns(1)
    qa_ref[...] = jnp.where(first_core, q_east, q_west)
    qb_ref[...] = jnp.where(first_core, q_west, q_east)


def stencil(w1_ref):
    return jnp.concatenate([w1_ref[3 * a + b] for b in range(3) for a in range(3)], axis=1)


def halves(w2_ref, w3_ref):
    return (w2_ref[...].astype(F32) * 0.5).astype(BF16), (w3_ref[...].astype(F32) * 0.5).astype(BF16)


def layers(w1, w2, w3, window):
    h = gelu_twice(jnp.dot(w1, window, preferred_element_type=F32)).astype(BF16)
    total = None
    for m in range(2):
        x = jnp.dot(w2[256 * m : 256 * m + 256], h, preferred_element_type=F32)
        y = gelu_twice(x).astype(BF16)
        part = jnp.dot(w3[:, 256 * m : 256 * m + 256], y, preferred_element_type=F32)
        total = part if total is None else total + part
    return 0.5 * total.astype(BF16).astype(F32)


GROUP = 4


def sweep(w1_ref, w2_ref, w3_ref, g_ref, fw, f0, fe, count, start):
    w1 = stencil(w1_ref)
    w2, w3 = halves(w2_ref, w3_ref)

    def step(g, carry):
        windows = []
        for i in range(GROUP):
            at = pl.multiple_of(16 * start(GROUP * g + i), 16)
            windows.append(jnp.concatenate([f[pl.ds(at, 48), :] for f in (fw, f0, fe)], axis=0))
        net = layers(w1, w2, w3, jnp.concatenate(windows, axis=1))
        for i in range(GROUP):
            at = pl.multiple_of(16 * (GROUP * g + i), 16)
            g_ref[pl.ds(at, 16), :] = net[:, 128 * i : 128 * i + 128]
        return carry

    lax.fori_loop(0, count // GROUP, step, 0)


def put(fw, f0, fe, at, x):
    n = x.shape[0]
    f0[at : at + n, :] = x.astype(BF16)
    fw[at : at + n, :] = roll(x, 1, 1).astype(BF16)
    fe[at : at + n, :] = roll(x, 127, 1).astype(BF16)


def middle_rows(fk_ref, w1_ref, w2_ref, w3_ref, g_ref, fw, f0, fe):
    put(fw, f0, fe, 0, fk_ref[16 * 7 : 16 * 41, :])
    sweep(w1_ref, w2_ref, w3_ref, g_ref, fw, f0, fe, 32, lambda i: i)


def outer_rows(fk_ref, fb_ref, w1_ref, w2_ref, w3_ref, g_ref, fw, f0, fe):
    put(fw, f0, fe, 0, fk_ref[16 * 39 : 16 * 63, :])
    put(fw, f0, fe, 16 * 24, fb_ref[32:64, :])
    put(fw, f0, fe, 16 * 26, fb_ref[0:32, :])
    put(fw, f0, fe, 16 * 28, fk_ref[16 : 16 * 9, :])
    sweep(w1_ref, w2_ref, w3_ref, g_ref, fw, f0, fe, 32, lambda i: i + jnp.where(i >= 24, 2, 0))


def closing(qa_ref, qb_ref, ha_ref, hb_ref, rf_ref, e4_ref, dd_ref, warm_ref, l_ref, d_ref,
            g1_ref, g2_ref, w1_ref, w2_ref, w3_ref, mix_ref, out_ref, eta_ref, mid_ref):
    first_core = lax.axis_index("lon") % 2 == 0
    ext = (80, 128)
    lane, row = iota(ext, 1), iota(ext, 0)
    qa, qb, ha, hb = qa_ref[...], qb_ref[...], ha_ref[...], hb_ref[...]
    q_west, q_east = jnp.where(first_core, qb, qa), jnp.where(first_core, qa, qb)
    h_west, h_east = jnp.where(first_core, hb, ha), jnp.where(first_core, ha, hb)
    mix = jnp.zeros(ext, F32)
    for k in range(16):
        mix = jnp.where(lane == k, mix_ref[k], mix)

    def delta(halo, own):
        return mix * roll(halo * own, 112, 1) * (halo - own)

    d_west, d_east = delta(h_west, q_west), delta(h_east, q_east)

    side = []
    for i in range(4):
        east = roll(h_east, 128 - (64 + 8 * i), 1)
        west = roll(h_west, 56 - 8 * i, 1)
        side.append(jnp.where(lane < 8, east, jnp.where(lane >= 120, west, 0.0)))
    main = [e4_ref[i] for i in range(4)]
    s_west = 0.01 * jnp.sum(d_west, axis=1, keepdims=True)
    s_east = 0.01 * jnp.sum(d_east, axis=1, keepdims=True)
    push = [main[0] + jnp.where(lane == 0, s_west, 0.0) + jnp.where(lane == 127, s_east, 0.0),
            side[0] - jnp.where(lane == 127, s_west, 0.0) - jnp.where(lane == 0, s_east, 0.0)]
    speed = [0.45 * x / 16 for x in (main[1], side[1])]
    current = [main[2], side[2]]
    earlier = [main[3], side[3]]

    def neighbours(pair):
        out = []
        for i in range(2):
            x, other = pair[i], pair[1 - i]
            out.append((roll(jnp.where(lane == 0, other, x), 127, 1),
                        roll(jnp.where(lane == 127, other, x), 1, 1),
                        roll(x, 79, 0), roll(x, 1, 0)))
        return out

    active = [jnp.where(s > 0.0, 1.0, 0.0).astype(F32) for s in speed]
    facing = [[jnp.minimum(s, n) for n in ns] for s, ns in zip(speed, neighbours(speed))]
    for _ in range(SUB):
        fresh = []
        for i, ns in enumerate(neighbours(current)):
            c = current[i]
            change = 2.0 * c - earlier[i] + push[i]
            for f, n in zip(facing[i], ns):
                change = change + f * (n - c)
            fresh.append(active[i] * change)
        current, earlier = fresh, current
    eta_ref[...] = current[0][8:72]
    mid_ref[...] = earlier[0][8:72]

    small = iota((8, 128), 1)
    rf = rf_ref[...]
    index_w = jnp.where(small < 64, 8 * (small & 15) + 3 + (small >> 4), 0)
    index_e = jnp.where(small < 64, 8 * (small & 15) + 1 + (small >> 4), 0)
    f_west = jnp.concatenate([lanes_from(rf[8 * i : 8 * i + 8], index_w) for i in range(10)], axis=0)
    f_east = jnp.concatenate([lanes_from(rf[8 * i : 8 * i + 8], index_e) for i in range(10)], axis=0)
    which = lane >> 4
    f_west = jnp.where(which == 0, roll(h_west, 96, 1) - d_west,
                       f_west + jnp.where(which == 1, roll(d_west, 16, 1), 0.0))
    f_east = jnp.where(which == 3, roll(h_east, 16, 1) - roll(d_east, 48, 1),
                       f_east + jnp.where(which == 2, roll(d_east, 32, 1), 0.0))
    cells = [f_east, roll(f_east, 112, 1), f_west, roll(f_west, 112, 1)]
    w2, w3 = halves(w2_ref, w3_ref)
    blank = jnp.zeros((128, 80), BF16)
    x = jnp.zeros((256, 128), F32)
    for a in range(3):
        window = jnp.concatenate([c[7 + a : 71 + a] for c in cells], axis=0).astype(BF16)
        w = jnp.concatenate([w1_ref[3 * a + b] for b in range(3)] + [blank], axis=1)
        x = x + lax.dot_general(window, w, NT, preferred_element_type=F32)
    h = gelu_twice(x).astype(BF16)
    y = gelu_twice(lax.dot_general(h, w2, NT, preferred_element_type=F32)).astype(BF16)
    w3 = jnp.concatenate([w3, jnp.zeros((112, 512), BF16)], axis=0)
    net = lax.dot_general(y, w3, NT, preferred_element_type=F32)
    net = 0.5 * net.astype(BF16).astype(F32)
    ends = [net[64 * c : 64 * c + 64] for c in range(4)]
    low16 = lane[:64] < 16
    ends[1] = ends[1] + jnp.where(low16, d_east[8:72], 0.0)
    ends[2] = ends[2] + jnp.where(low16, d_west[8:72], 0.0)
    spread = jnp.where(small < 64, small >> 2, 0)
    edges = []
    for i in range(8):
        x = jnp.zeros((8, 128), F32)
        for c in range(4):
            x = jnp.where(small & 3 == c, lanes_from(ends[c][8 * i : 8 * i + 8], spread), x)
        edges.append(x)

    at_edge = (small < 2) | (small >= 126)
    sub = iota((8, 128), 0)
    for i in range(8):
        depth = d_ref[8 * i : 8 * i + 8, :]
        for k in range(16):
            if i == 0:
                g = g2_ref[pl.ds(24 * 16 + k, 8, stride=16), :]
            elif i < 5:
                g = g1_ref[pl.ds((8 * i - 8) * 16 + k, 8, stride=16), :]
            else:
                g = g2_ref[pl.ds((8 * i - 40) * 16 + k, 8, stride=16), :]
            g = jnp.where(at_edge, roll(edges[i], 126 - 4 * k, 1), g)
            wet = jnp.where(k < depth, l_ref[k, 8 * i : 8 * i + 8, :].astype(F32), 0.0)
            y = warm_ref[k, 8 * i : 8 * i + 8, :] + wet * g
            if i == 0:
                y = y + jnp.where(sub == 0, dd_ref[k : k + 1, :], 0.0)
            if i == 7:
                y = y + jnp.where(sub == 7, dd_ref[16 + k : 17 + k, :], 0.0)
            out_ref[k, 8 * i : 8 * i + 8, :] = y


def partners(partner):
    pairs = []
    for lon in range(32):
        for lat in range(8):
            to = partner(lon, lat)
            pairs.append((8 * lon + lat, 8 * (to[0] % 32) + to[1]))
    return pairs


LAT_A = partners(lambda lon, lat: (lon, lat ^ 1))
LAT_B = partners(
    lambda lon, lat: (31 - lon, 7) if lat == 7 else (lon ^ 1, 0) if lat == 0 else (lon, lat + 1 if lat % 2 else lat - 1)
)
LON_A = partners(lambda lon, lat: (lon ^ 1, lat))
LON_B = partners(lambda lon, lat: (lon + 1 if lon % 2 else lon - 1, lat))


def swap(x, pairs):
    return lax.ppermute(x, ("lon", "lat"), pairs)


def on_device(t, now, prior, liquid, depth, mix, w1, w2, w3):
    warm, fk, fc, rt, rf, own, pa, pb = call(
        inside,
        (shape(16, 64, 128), shape(1024, 128), shape(2, 64, 128), shape(64, 128), shape(64, 128),
         shape(64, 128), shape(88, 128), shape(88, 128)),
        specs=[VM] * 5 + [SM], name="inside", flops=10**7, moved=2 * 10**6,
    )(t, liquid, depth, now, prior, mix)
    ra, rb = swap(pa, LAT_A), swap(pb, LAT_B)
    plane = [pltpu.VMEM((36 * 16, 128), BF16)] * 3
    g1 = call(middle_rows, shape(512, 128), scratch=plane, specs=[VM] * 4, name="middle_rows",
              flops=8 * 10**8, moved=10**6)(fk, w1, w2, w3)
    e4, fb, dd, rfx, qa, qb = call(
        between,
        (shape(4, 80, 128), shape(64, 128), shape(32, 128), shape(80, 128), shape(80, 128), shape(80, 128)),
        specs=[VM] * 9 + [SM], name="between", flops=10**7, moved=10**6,
    )(ra, rb, own, fk, fc, rt, rf, now, prior, mix)
    ha, hb = swap(qa, LON_A), swap(qb, LON_B)
    g2 = call(outer_rows, shape(512, 128), scratch=plane, specs=[VM] * 5, name="outer_rows",
              flops=8 * 10**8, moved=10**6)(fk, fb, w1, w2, w3)
    return call(
        closing,
        (shape(16, 64, 128), shape(64, 128), shape(64, 128)),
        specs=[VM] * 15 + [SM], name="closing", flops=10**8, moved=3 * 10**6,
    )(qa, qb, ha, hb, rfx, e4, dd, warm, liquid, depth, g1, g2, w1, w2, w3, mix)


def solution(mesh):
    wide, flat = P(None, "lat", "lon"), P("lat", "lon")
    return jax.shard_map(
        on_device,
        mesh=mesh,
        in_specs=(wide, flat, flat, wide, flat, P(), P(), P(), P()),
        out_specs=(wide, flat, flat),
        check_vma=False,
    )
```

profile of v0, /device:TPU:4, one launch (start us, length us, event | category | flops | bytes accessed | tf_op | source)
XLA Modules:
  0.0 36.9 jit_solution(18306384911605227698)
XLA Ops:
  0.6 0.0 copy-start
  0.6 1.0 %copy-done = s32[16,64,128]{2,1,0:T(8,128)S(1)} copy-done((s32[16,64,128]{2,1,0:T(8,128)S(1)}, s32[16,64,128]{2,1,0:T(8,128)}, u32[]{:S(2)}) %copy-start) | copy-done | bytes 524312
  1.7 0.0 copy-start.2
  1.7 1.0 %copy-done.2 = f32[16,64,128]{2,1,0:T(8,128)S(1)} copy-done((f32[16,64,128]{2,1,0:T(8,128)S(1)}, f32[16,64,128]{2,1,0:T(8,128)}, u32[]{:S(2)}) %copy-start.2) | copy-done | bytes 524312
  2.7 0.0 copy-start.3
  2.7 0.8 %copy-done.3 = s32[64,128]{1,0:T(8,128)S(1)} copy-done((s32[64,128]{1,0:T(8,128)S(1)}, s32[64,128]{1,0:T(8,128)}, u32[]{:S(2)}) %copy-start.3) | copy-done | bytes 32792
  3.5 0.0 copy-start.5
  3.5 0.8 %copy-done.5 = f32[64,128]{1,0:T(8,128)S(1)} copy-done((f32[64,128]{1,0:T(8,128)S(1)}, f32[64,128]{1,0:T(8,128)}, u32[]{:S(2)}) %copy-start.5) | copy-done | bytes 32792
  4.2 0.0 copy-start.7
  4.2 0.8 %copy-done.7 = f32[64,128]{1,0:T(8,128)S(1)} copy-done((f32[64,128]{1,0:T(8,128)S(1)}, f32[64,128]{1,0:T(8,128)}, u32[]{:S(2)}) %copy-start.7) | copy-done | bytes 32792
  5.0 0.0 copy-start.11
  5.0 0.7 %copy-done.11 = f32[16]{0:T(128)S(1)} copy-done((f32[16]{0:T(128)S(1)}, f32[16]{0:T(128)}, u32[]{:S(2)}) %copy-start.11) | copy-done | bytes 88
  5.6 0.0 copy-start.13
  5.7 2.4 %inside.1 = (f32[16,64,128]{2,1,0:T(8,128)S(1)}, f32[1024,128]{1,0:T(8,128)S(1)}, f32[2,64,128]{2,1,0:T(8,128)S(1)}, f32[64,128]{1,0:T(8,128)S(1)}, f32[64,128]{...) custom-call(f32[16,64,128]{2,1,0:T(8,128)S(1)} %copy-done.2, ...), custom_call_target="tpu_custom_call" | custom-call | flops 10000000 | bytes 2000000 | tf_op jit(solution)/shard_map/inside/pallas_call | solution.py:384
  8.1 1.7 %collective-permute-start = (f32[88,128]{1,0:T(8,128)S(1)}, f32[88,128]{1,0:T(8,128)S(1)}, u32[]{:S(2)}, u32[]{:S(2)}) collective-permute-start(f32[88,128]{1,0:T(8,128)S(1)} %get-tuple-element.17), channel_id=1, source_target_pairs={{0,1},{1,0},{2,3},{3,2},{4,5},{5,4},{6,7},{7,6},{8,9},{9,8},{10,11... | collective-permute-start | bytes 135176 | tf_op jit(solution)/shard_map/ppermute | solution.py:380
  9.8 0.0 copy-start.9
  9.8 0.0 copy-start.10
  9.8 2.1 %collective-permute-start.1 = (f32[88,128]{1,0:T(8,128)S(1)}, f32[88,128]{1,0:T(8,128)S(1)}, u32[]{:S(2)}, u32[]{:S(2)}) collective-permute-start(f32[88,128]{1,0:T(8,128)S(1)} %get-tuple-element.18), channel_id=1, source_target_pairs={{0,8},{1,2},{2,1},{3,4},{4,3},{5,6},{6,5},{7,255},{8,0},{9,10},{10... | collective-permute-start | bytes 135176 | tf_op jit(solution)/shard_map/ppermute | solution.py:380
  11.9 0.0 copy-done.13
  11.9 0.2 copy.12.w1_ref
  12.1 0.0 copy-done.9
  12.1 0.0 copy-done.10
  12.1 0.0 copy-start.6
  12.1 0.0 copy-start.8
  12.2 6.3 %middle_rows.1.g1_ref = f32[512,128]{1,0:T(8,128)S(1)} custom-call(f32[1024,128]{1,0:T(8,128)S(1)} %get-tuple-element.20.fk_ref, bf16[9,128,16]{2,1,0:T(8,128)(2,1)S(1)} %copy.12.w1_ref, bf16[512,128]{1,0:T(8,128)(2,1)S(1)} %copy-done.9, bf16[16,512]{1,0:T(8,128)(2,1)S(1)} %copy-done.10), custom_call_target="tpu_custom_call" | custom-call | flops 800000000 | bytes 1000000 | tf_op jit(solution)/shard_map/middle_rows/pallas_call | solution.py:392
  18.5 0.0 collective-permute-done.pa_ref
  18.5 0.0 collective-permute-done.1.pb_ref
  18.5 0.0 copy-start.12
  18.5 0.0 copy-done.6
  18.5 0.0 copy-done.8
  18.5 0.6 %copy-done.12 = f32[16]{0:T(128)S(1)} copy-done((f32[16]{0:T(128)S(1)}, f32[16]{0:T(128)}, u32[]{:S(2)}) %copy-start.12) | copy-done | bytes 88
  19.2 0.8 %between.1 = (f32[4,80,128]{2,1,0:T(8,128)S(1)}, f32[64,128]{1,0:T(8,128)S(1)}, f32[32,128]{1,0:T(8,128)S(1)}, f32[80,128]{1,0:T(8,128)S(1)}, f32[80,128]{1,0:T(8,128)S(1)}, /*index=5*/f32[80,128]{1,0:T(8,128)S(1)}) custom-call(f32[88,128]{1,0:T(8,128)S(1)} %collective-permute-done.pa_ref, f32[88,128]{1,0:T(8,128)S(1)} %collective-permute-done.1.pb_ref, ...), custom_call_target="tpu_custom_call" | custom-call | flops 10000000 | bytes 1000000 | tf_op jit(solution)/shard_map/between/pallas_call | solution.py:394
  19.9 0.1 collective-permute-start.2
  20.0 7.5 %collective-permute-start.3 = (f32[80,128]{1,0:T(8,128)S(1)}, f32[80,128]{1,0:T(8,128)S(1)}, u32[]{:S(2)}, u32[]{:S(2)}) collective-permute-start(f32[80,128]{1,0:T(8,128)S(1)} %get-tuple-element.25.qb_ref), channel_id=1, source_target_pairs={{0,248},{1,249},{2,250},{3,251},{4,252},{5,253},{6,254},{7,255},{8... | collective-permute-start | bytes 122888 | tf_op jit(solution)/shard_map/ppermute | solution.py:380
  27.5 0.0 copy-start.1
  27.5 0.0 copy-start.4
  27.5 6.3 %outer_rows.1.g2_ref = f32[512,128]{1,0:T(8,128)S(1)} custom-call(f32[1024,128]{1,0:T(8,128)S(1)} %get-tuple-element.20.fk_ref, f32[64,128]{1,0:T(8,128)S(1)} %get-tuple-element.30.fb_ref, bf16[9,128,16]{2,1,0:T(8,128)(2,1)S(1)} %copy.12.w1_ref, bf16[512,128]{1,0:T(8,128)(2,1)S(1)} %copy-done.9, bf16[16,512]{1,0:T(8,128)(2,1)S(1)} %copy-done.10), custom_call_target="tpu_custom_call" | custom-call | flops 800000000 | bytes 1000000 | tf_op jit(solution)/shard_map/outer_rows/pallas_call | solution.py:400
  33.8 0.0 collective-permute-done.2.ha_ref
  33.8 0.0 collective-permute-done.3.hb_ref
  33.8 0.0 copy-done.1
  33.8 0.0 copy-done.4
  33.9 3.1 %closing.1 = (f32[16,64,128]{2,1,0:T(8,128)}, f32[64,128]{1,0:T(8,128)}, f32[64,128]{1,0:T(8,128)}) custom-call(f32[80,128]{1,0:T(8,128)S(1)} %get-tuple-element.24.qa_ref, f32[80,128]{1,0:T(8,128)S(1)} %get-tuple-element.25.qb_ref, f32[80,128]{1,0:T(8,128)S(1)} %collective-permute-done.2.ha_ref, f32[80,128]{1,0:T(8,128)S(1)} %collective-permute-done.3.hb_ref, ...), custom_call_target="tpu_custom_call" | custom-call | flops 100000000 | bytes 3000000 | tf_op jit(solution)/shard_map/closing/pallas_call | solution.py:402
Async XLA Ops:
  0.6 1.0 %copy-start = (s32[16,64,128]{2,1,0:T(8,128)S(1)}, s32[16,64,128]{2,1,0:T(8,128)}, u32[]{:S(2)}) copy-start(s32[16,64,128]{2,1,0:T(8,128)} %l_ref.3) | copy-start | bytes 1572868
  1.7 1.0 %copy-start.2 = (f32[16,64,128]{2,1,0:T(8,128)S(1)}, f32[16,64,128]{2,1,0:T(8,128)}, u32[]{:S(2)}) copy-start(f32[16,64,128]{2,1,0:T(8,128)} %t_ref.1) | copy-start | bytes 1572868
  2.7 0.8 %copy-start.3 = (s32[64,128]{1,0:T(8,128)S(1)}, s32[64,128]{1,0:T(8,128)}, u32[]{:S(2)}) copy-start(s32[64,128]{1,0:T(8,128)} %d_ref.3) | copy-start | bytes 98308
  3.5 0.8 %copy-start.5 = (f32[64,128]{1,0:T(8,128)S(1)}, f32[64,128]{1,0:T(8,128)}, u32[]{:S(2)}) copy-start(f32[64,128]{1,0:T(8,128)} %now_ref.3) | copy-start | bytes 98308
  4.2 0.8 %copy-start.7 = (f32[64,128]{1,0:T(8,128)S(1)}, f32[64,128]{1,0:T(8,128)}, u32[]{:S(2)}) copy-start(f32[64,128]{1,0:T(8,128)} %prior_ref.3) | copy-start | bytes 98308
  5.0 0.7 %copy-start.11 = (f32[16]{0:T(128)S(1)}, f32[16]{0:T(128)}, u32[]{:S(2)}) copy-start(f32[16]{0:T(128)} %mix_ref.5) | copy-start | bytes 196
  5.6 6.2 %copy-start.13 = (bf16[9,128,16]{1,2,0:T(8,128)(2,1)S(1)}, bf16[9,128,16]{1,2,0:T(8,128)(2,1)}, u32[]{:S(2)}) copy-start(bf16[9,128,16]{1,2,0:T(8,128)(2,1)} %param.15) | copy-start | bytes 110596
  8.1 10.4 %collective-permute-start = (f32[88,128]{1,0:T(8,128)S(1)}, f32[88,128]{1,0:T(8,128)S(1)}, u32[]{:S(2)}, u32[]{:S(2)}) collective-permute-start(f32[88,128]{1,0:T(8,128)S(1)} %get-tuple-element.17), channel_id=1, source_target_pairs={{0,1},{1,0},{2,3},{3,2},{4,5},{5,4},{6,7},{7,6},{8,9},{9,8},{10,11... | collective-permute-start | bytes 135176 | tf_op jit(solution)/shard_map/ppermute | solution.py:380
  9.8 2.4 %copy-start.9 = (bf16[512,128]{1,0:T(8,128)(2,1)S(1)}, bf16[512,128]{1,0:T(8,128)(2,1)}, u32[]{:S(2)}) copy-start(bf16[512,128]{1,0:T(8,128)(2,1)} %w2_ref.5) | copy-start | bytes 393220
  9.8 2.4 %copy-start.10 = (bf16[16,512]{1,0:T(8,128)(2,1)S(1)}, bf16[16,512]{1,0:T(8,128)(2,1)}, u32[]{:S(2)}) copy-start(bf16[16,512]{1,0:T(8,128)(2,1)} %w3_ref.5) | copy-start | bytes 49156
  9.8 8.7 %collective-permute-start.1 = (f32[88,128]{1,0:T(8,128)S(1)}, f32[88,128]{1,0:T(8,128)S(1)}, u32[]{:S(2)}, u32[]{:S(2)}) collective-permute-start(f32[88,128]{1,0:T(8,128)S(1)} %get-tuple-element.18), channel_id=1, source_target_pairs={{0,8},{1,2},{2,1},{3,4},{4,3},{5,6},{6,5},{7,255},{8,0},{9,10},{10... | collective-permute-start | bytes 135176 | tf_op jit(solution)/shard_map/ppermute | solution.py:380
  12.1 6.4 %copy-start.6 = (f32[64,128]{1,0:T(8,128)S(1)}, f32[64,128]{1,0:T(8,128)}, u32[]{:S(2)}) copy-start(f32[64,128]{1,0:T(8,128)} %now_ref.3) | copy-start | bytes 98308
  12.1 6.4 %copy-start.8 = (f32[64,128]{1,0:T(8,128)S(1)}, f32[64,128]{1,0:T(8,128)}, u32[]{:S(2)}) copy-start(f32[64,128]{1,0:T(8,128)} %prior_ref.3) | copy-start | bytes 98308
  18.5 0.7 %copy-start.12 = (f32[16]{0:T(128)S(1)}, f32[16]{0:T(128)}, u32[]{:S(2)}) copy-start(f32[16]{0:T(128)} %mix_ref.5) | copy-start | bytes 196
  19.9 13.9 %collective-permute-start.2 = (f32[80,128]{1,0:T(8,128)S(1)}, f32[80,128]{1,0:T(8,128)S(1)}, u32[]{:S(2)}, u32[]{:S(2)}) collective-permute-start(f32[80,128]{1,0:T(8,128)S(1)} %get-tuple-element.24.qa_ref), channel_id=1, source_target_pairs={{0,8},{1,9},{2,10},{3,11},{4,12},{5,13},{6,14},{7,15},{8,0},{9,1},... | collective-permute-start | bytes 122888 | tf_op jit(solution)/shard_map/ppermute | solution.py:380
  20.0 13.8 %collective-permute-start.3 = (f32[80,128]{1,0:T(8,128)S(1)}, f32[80,128]{1,0:T(8,128)S(1)}, u32[]{:S(2)}, u32[]{:S(2)}) collective-permute-start(f32[80,128]{1,0:T(8,128)S(1)} %get-tuple-element.25.qb_ref), channel_id=1, source_target_pairs={{0,248},{1,249},{2,250},{3,251},{4,252},{5,253},{6,254},{7,255},{8... | collective-permute-start | bytes 122888 | tf_op jit(solution)/shard_map/ppermute | solution.py:380
  27.5 6.3 %copy-start.1 = (s32[16,64,128]{2,1,0:T(8,128)S(1)}, s32[16,64,128]{2,1,0:T(8,128)}, u32[]{:S(2)}) copy-start(s32[16,64,128]{2,1,0:T(8,128)} %l_ref.3) | copy-start | bytes 1572868
  27.5 6.3 %copy-start.4 = (s32[64,128]{1,0:T(8,128)S(1)}, s32[64,128]{1,0:T(8,128)}, u32[]{:S(2)}) copy-start(s32[64,128]{1,0:T(8,128)} %d_ref.3) | copy-start | bytes 98308
where the time goes:
time: 37.4 us; the launch traced here: 36.9 us
  Pallas kernels  18.9 us (51%)
  starting transfers between devices  11.4 us (30%)
  local copies, waits for them, and re-layouts  5.89 us (16%)
  between operations  0.77 us (2%)
    ppermute x4, starting transfers between devices, swap(): return lax.ppermute(x, ('lon', 'lat'), pairs)  11.4 us
    pallas_call x1, Pallas kernels, on_device(): call(middle_rows, shape(512, 128), scratch=plane, specs=[VM] * 4, name='m...  6.33 us
    pallas_call x1, Pallas kernels, on_device(): call(outer_rows, shape(512, 128), scratch=plane, specs=[VM] * 5, name='ou...  6.27 us
    unnamed x29, local copies, waits for them, and re-layouts  5.89 us
    pallas_call x1, Pallas kernels, on_device(): call(closing, (shape(16, 64, 128), shape(64, 128), shape(64, 128)), specs...  3.08 us
    pallas_call x1, Pallas kernels, on_device(): call(inside, (shape(16, 64, 128), shape(1024, 128), shape(2, 64, 128), sh...  2.44 us
    pallas_call x1, Pallas kernels, on_device(): call(between, (shape(4, 80, 128), shape(64, 128), shape(32, 128), shape(8...  0.77 us
  transfers between devices with their start and end apart: 4, of which 0 were waited for; matrix products, arithmetic and copies ran while one was open for 1% of the time, Pallas kernels for 34%

commit v1 on v0

--- a/solution.py
+++ b/solution.py
@@ -11,7 +11,7 @@
 C0 = 0.7978845608028654
 C1 = 0.044715 * C0
 VM = pl.BlockSpec(memory_space=pltpu.VMEM)
-SM = pl.BlockSpec(memory_space=pltpu.SMEM)
+HB = pl.BlockSpec(memory_space=pltpu.HBM)
 NT = (((1,), (1,)), ((), ()))
 
 
@@ -33,14 +33,14 @@
     return x + x * jnp.tanh(x * (C0 + C1 * (x * x)))
 
 
-def call(body, outs, scratch=(), specs=None, flops=0, moved=0, **given):
+def call(body, outs, scratch=(), specs=None, out_specs=None, flops=0, moved=0, room=40, **given):
     return pl.pallas_call(
         body,
         out_shape=outs,
         in_specs=specs,
-        out_specs=jax.tree.map(lambda _: VM, outs),
+        out_specs=out_specs or jax.tree.map(lambda _: VM, outs),
         scratch_shapes=list(scratch),
-        compiler_params=pltpu.CompilerParams(vmem_limit_bytes=40 * 1024 * 1024),
+        compiler_params=pltpu.CompilerParams(vmem_limit_bytes=room * 1024 * 1024),
         cost_estimate=pl.CostEstimate(flops=flops, bytes_accessed=moved, transcendentals=0),
         **given,
     )
@@ -50,9 +50,21 @@
     return jax.ShapeDtypeStruct(dims, dtype)
 
 
-def inside(t_ref, l_ref, d_ref, now_ref, prior_ref, mix_ref,
-           warm_ref, fk_ref, fc_ref, rt_ref, rf_ref, own_ref, pa_ref, pb_ref):
+def inside(t_hbm, l_hbm, d_hbm, now_hbm, prior_hbm, mix_hbm,
+           warm_ref, wet_ref, fk_ref, fc_ref, rt_ref, rf_ref, own_ref, np_ref, mx_ref, pa_ref, pb_ref,
+           t_ref, l_ref, d_ref, mix_ref, sems):
     lat = lax.axis_index("lat")
+    copies = [pltpu.make_async_copy(d_hbm, d_ref, sems.at[0]), pltpu.make_async_copy(mix_hbm, mix_ref, sems.at[1])]
+    for c in range(4):
+        part = pl.ds(4 * c, 4)
+        copies.append(pltpu.make_async_copy(t_hbm.at[part], t_ref.at[part], sems.at[2 + 2 * c]))
+        copies.append(pltpu.make_async_copy(l_hbm.at[part], l_ref.at[part], sems.at[3 + 2 * c]))
+    copies.append(pltpu.make_async_copy(now_hbm, np_ref.at[0], sems.at[10]))
+    copies.append(pltpu.make_async_copy(prior_hbm, np_ref.at[1], sems.at[11]))
+    for copy in copies:
+        copy.start()
+    copies[0].wait()
+    copies[1].wait()
     dims = (64, 128)
     lane, row = iota(dims, 1), iota(dims, 0)
     depth = d_ref[...]
@@ -69,8 +81,12 @@
         return (east + west) + (north + south)
 
     for k in range(16):
+        if k % 4 == 0:
+            copies[2 + k // 2].wait()
+            copies[3 + k // 2].wait()
         t = t_ref[k]
         wet = jnp.where(k < depth, l_ref[k].astype(F32), 0.0)
+        wet_ref[k] = wet
         warm = t + (mix_ref[k] * wet) * (around(wet * t) - t * around(wet))
         feature = wet * warm
         warm_ref[k] = warm
@@ -86,16 +102,18 @@
     rt_ref[...] = rt
     rf_ref[...] = rf
 
-    level = iota((16, 128), 0)
-
-    def edge(r):
-        wet = jnp.where(level < d_ref[r : r + 1, :], l_ref[:, r, :].astype(F32), 0.0)
-        return t_ref[:, r, :], wet, fk_ref[16 * r : 16 * r + 16, :]
+    copies[10].wait()
+    copies[11].wait()
+    level, lane16 = iota((24, 128), 0), iota((24, 128), 1)
+    mx = jnp.zeros((24, 128), F32)
+    for k in range(16):
+        mx = jnp.where((level == k) | ((level == 16) & (lane16 == k)), mix_ref[k], mx)
+    mx_ref[...] = mx
 
     def payload(r, first):
-        t, wet, feature = edge(r)
-        own = jnp.concatenate([t, wet], axis=0)
-        rows = [x[first : first + 8] for x in (forcing, column, now_ref[...], prior_ref[...], rt)]
+        own = jnp.concatenate([t_ref[:, r, :], wet_ref[:, r, :]], axis=0)
+        feature = fk_ref[16 * r : 16 * r + 16, :]
+        rows = [x[first : first + 8] for x in (forcing, column, np_ref[0], np_ref[1], rt)]
         return own, jnp.concatenate([own, feature] + rows, axis=0)
 
     own_low, low = payload(0, 0)
@@ -118,7 +136,7 @@
             pb_ref[8 * i : 8 * i + 8, :] = x
 
 
-def between(pa_ref, pb_ref, own_ref, fk_ref, fc_ref, rt_ref, rf_ref, now_ref, prior_ref, mix_ref,
+def between(pa_ref, pb_ref, own_ref, fk_ref, fc_ref, rt_ref, rf_ref, np_ref, mx_ref,
             e4_ref, fb_ref, dd_ref, rfx_ref, qa_ref, qb_ref):
     lat = lax.axis_index("lat")
     even = lat % 2 == 0
@@ -126,9 +144,7 @@
     high = jnp.where(even, pa, pb)
     low = jnp.where(lat == 0, 0.0, jnp.where(even, pb, pa))
     level, lane16 = iota((16, 128), 0), iota((16, 128), 1)
-    mix = jnp.zeros((16, 128), F32)
-    for k in range(16):
-        mix = jnp.where(level == k, mix_ref[k], mix)
+    mix = mx_ref[0:16, :]
 
     def delta(halo, first):
         t, wet = own_ref[first : first + 16, :], own_ref[first + 16 : first + 32, :]
@@ -153,7 +169,7 @@
     forcing = extend(0, fc_ref[0])
     forcing = forcing + jnp.where(row == 8, s_low, 0.0) - jnp.where(row == 7, s_low, 0.0)
     forcing = forcing + jnp.where(row == 71, s_high, 0.0) - jnp.where(row == 72, s_high, 0.0)
-    fields = [forcing, extend(1, fc_ref[1]), extend(2, now_ref[...]), extend(3, prior_ref[...])]
+    fields = [forcing, extend(1, fc_ref[1]), extend(2, np_ref[0]), extend(3, np_ref[1])]
     mixed = extend(4, rt_ref[...])
     for i, field in enumerate(fields):
         e4_ref[i] = field
@@ -198,34 +214,25 @@
 
 def layers(w1, w2, w3, window):
     h = gelu_twice(jnp.dot(w1, window, preferred_element_type=F32)).astype(BF16)
-    total = None
-    for m in range(2):
-        x = jnp.dot(w2[256 * m : 256 * m + 256], h, preferred_element_type=F32)
-        y = gelu_twice(x).astype(BF16)
-        part = jnp.dot(w3[:, 256 * m : 256 * m + 256], y, preferred_element_type=F32)
-        total = part if total is None else total + part
-    return 0.5 * total.astype(BF16).astype(F32)
-
-
-GROUP = 4
-
-
-def sweep(w1_ref, w2_ref, w3_ref, g_ref, fw, f0, fe, count, start):
+    y = gelu_twice(jnp.dot(w2, h, preferred_element_type=F32)).astype(BF16)
+    net = jnp.dot(w3, y, preferred_element_type=F32)
+    return 0.5 * net.astype(BF16).astype(F32)
+
+
+GROUP = 16
+
+
+def sweep(w1_ref, w2_ref, w3_ref, g_ref, fw, f0, fe, starts):
     w1 = stencil(w1_ref)
     w2, w3 = halves(w2_ref, w3_ref)
-
-    def step(g, carry):
-        windows = []
-        for i in range(GROUP):
-            at = pl.multiple_of(16 * start(GROUP * g + i), 16)
-            windows.append(jnp.concatenate([f[pl.ds(at, 48), :] for f in (fw, f0, fe)], axis=0))
+    for g in range(0, len(starts), GROUP):
+        windows = [
+            jnp.concatenate([f[16 * at : 16 * at + 48, :] for f in (fw, f0, fe)], axis=0)
+            for at in starts[g : g + GROUP]
+        ]
         net = layers(w1, w2, w3, jnp.concatenate(windows, axis=1))
         for i in range(GROUP):
-            at = pl.multiple_of(16 * (GROUP * g + i), 16)
-            g_ref[pl.ds(at, 16), :] = net[:, 128 * i : 128 * i + 128]
-        return carry
-
-    lax.fori_loop(0, count // GROUP, step, 0)
+            g_ref[16 * (g + i) : 16 * (g + i) + 16, :] = net[:, 128 * i : 128 * i + 128]
 
 
 def put(fw, f0, fe, at, x):
@@ -237,7 +244,7 @@
 
 def middle_rows(fk_ref, w1_ref, w2_ref, w3_ref, g_ref, fw, f0, fe):
     put(fw, f0, fe, 0, fk_ref[16 * 7 : 16 * 41, :])
-    sweep(w1_ref, w2_ref, w3_ref, g_ref, fw, f0, fe, 32, lambda i: i)
+    sweep(w1_ref, w2_ref, w3_ref, g_ref, fw, f0, fe, list(range(32)))
 
 
 def outer_rows(fk_ref, fb_ref, w1_ref, w2_ref, w3_ref, g_ref, fw, f0, fe):
@@ -245,20 +252,18 @@
     put(fw, f0, fe, 16 * 24, fb_ref[32:64, :])
     put(fw, f0, fe, 16 * 26, fb_ref[0:32, :])
     put(fw, f0, fe, 16 * 28, fk_ref[16 : 16 * 9, :])
-    sweep(w1_ref, w2_ref, w3_ref, g_ref, fw, f0, fe, 32, lambda i: i + jnp.where(i >= 24, 2, 0))
-
-
-def closing(qa_ref, qb_ref, ha_ref, hb_ref, rf_ref, e4_ref, dd_ref, warm_ref, l_ref, d_ref,
-            g1_ref, g2_ref, w1_ref, w2_ref, w3_ref, mix_ref, out_ref, eta_ref, mid_ref):
+    sweep(w1_ref, w2_ref, w3_ref, g_ref, fw, f0, fe, [i + 2 * (i >= 24) for i in range(32)])
+
+
+def closing(qa_ref, qb_ref, ha_ref, hb_ref, rf_ref, e4_ref, dd_ref, warm_ref, wet_ref,
+            g1_ref, g2_ref, w1_ref, w2_ref, w3_ref, mx_ref, out_hbm, eta_ref, mid_ref, out_ref, sems):
     first_core = lax.axis_index("lon") % 2 == 0
     ext = (80, 128)
     lane, row = iota(ext, 1), iota(ext, 0)
     qa, qb, ha, hb = qa_ref[...], qb_ref[...], ha_ref[...], hb_ref[...]
     q_west, q_east = jnp.where(first_core, qb, qa), jnp.where(first_core, qa, qb)
     h_west, h_east = jnp.where(first_core, hb, ha), jnp.where(first_core, ha, hb)
-    mix = jnp.zeros(ext, F32)
-    for k in range(16):
-        mix = jnp.where(lane == k, mix_ref[k], mix)
+    mix = mx_ref[16:17, :]
 
     def delta(halo, own):
         return mix * roll(halo * own, 112, 1) * (halo - own)
@@ -340,9 +345,9 @@
 
     at_edge = (small < 2) | (small >= 126)
     sub = iota((8, 128), 0)
-    for i in range(8):
-        depth = d_ref[8 * i : 8 * i + 8, :]
-        for k in range(16):
+    copies = []
+    for k in range(16):
+        for i in range(8):
             if i == 0:
                 g = g2_ref[pl.ds(24 * 16 + k, 8, stride=16), :]
             elif i < 5:
@@ -350,13 +355,18 @@
             else:
                 g = g2_ref[pl.ds((8 * i - 40) * 16 + k, 8, stride=16), :]
             g = jnp.where(at_edge, roll(edges[i], 126 - 4 * k, 1), g)
-            wet = jnp.where(k < depth, l_ref[k, 8 * i : 8 * i + 8, :].astype(F32), 0.0)
-            y = warm_ref[k, 8 * i : 8 * i + 8, :] + wet * g
+            y = warm_ref[k, 8 * i : 8 * i + 8, :] + wet_ref[k, 8 * i : 8 * i + 8, :] * g
             if i == 0:
                 y = y + jnp.where(sub == 0, dd_ref[k : k + 1, :], 0.0)
             if i == 7:
                 y = y + jnp.where(sub == 7, dd_ref[16 + k : 17 + k, :], 0.0)
             out_ref[k, 8 * i : 8 * i + 8, :] = y
+        if k % 4 == 3:
+            part = pl.ds(k - 3, 4)
+            copies.append(pltpu.make_async_copy(out_ref.at[part], out_hbm.at[part], sems.at[k // 4]))
+            copies[-1].start()
+    for copy in copies:
+        copy.wait()
 
 
 def partners(partner):
@@ -381,29 +391,33 @@
 
 
 def on_device(t, now, prior, liquid, depth, mix, w1, w2, w3):
-    warm, fk, fc, rt, rf, own, pa, pb = call(
+    cube, flat, tall = (16, 64, 128), (64, 128), (80, 128)
+    warm, wet, fk, fc, rt, rf, own, both, mx, pa, pb = call(
         inside,
-        (shape(16, 64, 128), shape(1024, 128), shape(2, 64, 128), shape(64, 128), shape(64, 128),
-         shape(64, 128), shape(88, 128), shape(88, 128)),
-        specs=[VM] * 5 + [SM], name="inside", flops=10**7, moved=2 * 10**6,
-    )(t, liquid, depth, now, prior, mix)
+        (shape(*cube), shape(*cube), shape(1024, 128), shape(2, 64, 128), shape(*flat), shape(*flat),
+         shape(*flat), shape(2, 64, 128), shape(24, 128), shape(88, 128), shape(88, 128)),
+        scratch=(pltpu.VMEM(cube, F32), pltpu.VMEM(cube, jnp.int32), pltpu.VMEM(flat, jnp.int32),
+                 pltpu.SMEM((16,), F32), pltpu.SemaphoreType.DMA((12,))),
+        specs=[HB] * 6, name="inside", flops=10**7, moved=2 * 10**6,
+    )(*(pltpu.with_memory_space_constraint(x, pltpu.HBM) for x in (t, liquid, depth, now, prior, mix)))
     ra, rb = swap(pa, LAT_A), swap(pb, LAT_B)
     plane = [pltpu.VMEM((36 * 16, 128), BF16)] * 3
     g1 = call(middle_rows, shape(512, 128), scratch=plane, specs=[VM] * 4, name="middle_rows",
               flops=8 * 10**8, moved=10**6)(fk, w1, w2, w3)
     e4, fb, dd, rfx, qa, qb = call(
         between,
-        (shape(4, 80, 128), shape(64, 128), shape(32, 128), shape(80, 128), shape(80, 128), shape(80, 128)),
-        specs=[VM] * 9 + [SM], name="between", flops=10**7, moved=10**6,
-    )(ra, rb, own, fk, fc, rt, rf, now, prior, mix)
+        (shape(4, 80, 128), shape(64, 128), shape(32, 128), shape(*tall), shape(*tall), shape(*tall)),
+        specs=[VM] * 9, name="between", flops=10**7, moved=10**6,
+    )(ra, rb, own, fk, fc, rt, rf, both, mx)
     ha, hb = swap(qa, LON_A), swap(qb, LON_B)
     g2 = call(outer_rows, shape(512, 128), scratch=plane, specs=[VM] * 5, name="outer_rows",
               flops=8 * 10**8, moved=10**6)(fk, fb, w1, w2, w3)
     return call(
         closing,
-        (shape(16, 64, 128), shape(64, 128), shape(64, 128)),
-        specs=[VM] * 15 + [SM], name="closing", flops=10**8, moved=3 * 10**6,
-    )(qa, qb, ha, hb, rfx, e4, dd, warm, liquid, depth, g1, g2, w1, w2, w3, mix)
+        (shape(*cube), shape(*flat), shape(*flat)),
+        scratch=(pltpu.VMEM(cube, F32), pltpu.SemaphoreType.DMA((4,))),
+        specs=[VM] * 15, out_specs=(HB, VM, VM), name="closing", flops=10**8, moved=3 * 10**6,
+    )(qa, qb, ha, hb, rfx, e4, dd, warm, wet, g1, g2, w1, w2, w3, mx)
 
 
 def solution(mesh):

time: 37.4 us -> 26.5 us (0.71); the launches traced: 36.9 us -> 26.4 us
  Pallas kernels: 18.9 us -> 13 us
  local copies, waits for them, and re-layouts: 5.89 us -> 0.23 us
  waiting for transfers between devices: 0.02 us -> 1.99 us
  starting transfers between devices: 11.4 us -> 10.5 us
    unnamed x29 -> x7, local copies, waits for them, and re-layouts: 5.89 us -> 0.23 us
    pallas_call x1, Pallas kernels: 6.33 us -> 3.31 us  [on_device(): call(middle_rows, shape(512, 128), scratch=plane, specs=[VM] * 4, name='m...]
    pallas_call x1, Pallas kernels: 6.27 us -> 3.31 us  [on_device(): call(outer_rows, shape(512, 128), scratch=plane, specs=[VM] * 5, name='ou...]
    ppermute x4, waiting for transfers between devices: 0.02 us -> 1.99 us  [swap(): return lax.ppermute(x, ('lon', 'lat'), pairs)]
    ppermute x4, starting transfers between devices: 11.4 us -> 10.5 us  [swap(): return lax.ppermute(x, ('lon', 'lat'), pairs)]
  transfers between devices with their start and end apart: 4 -> 4, of which waited for: 0 -> 1; matrix products, arithmetic and copies ran while one was open for 1% -> 1% of each run, Pallas kernels for 34% -> 25%
where the time goes in v1:
time: 26.5 us; the launch traced here: 26.4 us
  Pallas kernels  13 us (49%)
  starting transfers between devices  10.5 us (40%)
  waiting for transfers between devices  1.99 us (8%)
  between operations  0.71 us (3%)
    ppermute x4, starting transfers between devices, swap(): return lax.ppermute(x, ('lon', 'lat'), pairs)  10.5 us
    pallas_call x1, Pallas kernels, on_device(): call(outer_rows, shape(512, 128), scratch=plane, specs=[VM] * 5, name='ou...  3.31 us
    pallas_call x1, Pallas kernels, on_device(): call(middle_rows, shape(512, 128), scratch=plane, specs=[VM] * 4, name='m...  3.31 us
    pallas_call x1, Pallas kernels, on_device(): call(closing, (shape(*cube), shape(*flat), shape(*flat)), scratch=(pltpu....  3.22 us
    pallas_call x1, Pallas kernels, on_device(): call(inside, (shape(*cube), shape(*cube), shape(1024, 128), shape(2, 64,...  2.96 us
    ppermute x4, waiting for transfers between devices, swap(): return lax.ppermute(x, ('lon', 'lat'), pairs)  1.99 us
  transfers between devices with their start and end apart: 4, of which 1 were waited for; matrix products, arithmetic and copies ran while one was open for 1% of the time, Pallas kernels for 25%

profile of v1, /device:TPU:4, one launch (start us, length us, event | category | flops | bytes accessed | tf_op | source)
XLA Modules:
  0.0 26.4 jit_solution(2814626867362134469)
XLA Ops:
  0.6 0.0 copy-start.2
  0.6 3.0 %inside.1 = (f32[16,64,128]{2,1,0:T(8,128)S(1)}, f32[16,64,128]{2,1,0:T(8,128)S(1)}, f32[1024,128]{1,0:T(8,128)S(1)}, f32[2,64,128]{2,1,0:T(8,128)S(1)}, f32[64,...) custom-call(f32[16,64,128]{2,1,0:T(8,128)} %t_hbm.1, ...), custom_call_target="tpu_custom_call" | custom-call | flops 10000000 | bytes 2000000 | tf_op jit(solution)/shard_map/inside/pallas_call | solution.py:395
  3.6 1.7 %collective-permute-start = (f32[88,128]{1,0:T(8,128)S(1)}, f32[88,128]{1,0:T(8,128)S(1)}, u32[]{:S(2)}, u32[]{:S(2)}) collective-permute-start(f32[88,128]{1,0:T(8,128)S(1)} %get-tuple-element.20), channel_id=1, source_target_pairs={{0,1},{1,0},{2,3},{3,2},{4,5},{5,4},{6,7},{7,6},{8,9},{9,8},{10,11... | collective-permute-start | bytes 135176 | tf_op jit(solution)/shard_map/ppermute | solution.py:390
  5.3 0.0 copy-start
  5.3 0.0 copy-start.1
  5.3 2.1 %collective-permute-start.1 = (f32[88,128]{1,0:T(8,128)S(1)}, f32[88,128]{1,0:T(8,128)S(1)}, u32[]{:S(2)}, u32[]{:S(2)}) collective-permute-start(f32[88,128]{1,0:T(8,128)S(1)} %get-tuple-element.21), channel_id=1, source_target_pairs={{0,8},{1,2},{2,1},{3,4},{4,3},{5,6},{6,5},{7,255},{8,0},{9,10},{10... | collective-permute-start | bytes 135176 | tf_op jit(solution)/shard_map/ppermute | solution.py:390
  7.4 0.0 copy-done.2
  7.4 0.2 copy.12.w1_ref
  7.6 0.0 copy-done
  7.6 0.0 copy-done.1
  7.6 3.3 %middle_rows.1.g1_ref = f32[512,128]{1,0:T(8,128)S(1)} custom-call(f32[1024,128]{1,0:T(8,128)S(1)} %get-tuple-element.23.fk_ref, bf16[9,128,16]{2,1,0:T(8,128)(2,1)S(1)} %copy.12.w1_ref, bf16[512,128]{1,0:T(8,128)(2,1)S(1)} %copy-done, bf16[16,512]{1,0:T(8,128)(2,1)S(1)} %copy-done.1), custom_call_target="tpu_custom_call" | custom-call | flops 800000000 | bytes 1000000 | tf_op jit(solution)/shard_map/middle_rows/pallas_call | solution.py:405
  11.0 0.0 collective-permute-done.pa_ref
  11.0 2.0 %collective-permute-done.1.pb_ref = f32[88,128]{1,0:T(8,128)S(1)} collective-permute-done((f32[88,128]{1,0:T(8,128)S(1)}, f32[88,128]{1,0:T(8,128)S(1)}, u32[]{:S(2)}, u32[]{:S(2)}) %collective-permute-start.1) | collective-permute-done | bytes 45088 | tf_op jit(solution)/shard_map/ppermute | solution.py:390
  12.9 0.2 between.1
  13.2 0.1 collective-permute-start.2
  13.3 6.6 %collective-permute-start.3 = (f32[80,128]{1,0:T(8,128)S(1)}, f32[80,128]{1,0:T(8,128)S(1)}, u32[]{:S(2)}, u32[]{:S(2)}) collective-permute-start(f32[80,128]{1,0:T(8,128)S(1)} %get-tuple-element.30.qb_ref), channel_id=1, source_target_pairs={{0,248},{1,249},{2,250},{3,251},{4,252},{5,253},{6,254},{7,255},{8... | collective-permute-start | bytes 122888 | tf_op jit(solution)/shard_map/ppermute | solution.py:390
  19.9 3.3 %outer_rows.1.g2_ref = f32[512,128]{1,0:T(8,128)S(1)} custom-call(f32[1024,128]{1,0:T(8,128)S(1)} %get-tuple-element.23.fk_ref, f32[64,128]{1,0:T(8,128)S(1)} %get-tuple-element.36.fb_ref, bf16[9,128,16]{2,1,0:T(8,128)(2,1)S(1)} %copy.12.w1_ref, bf16[512,128]{1,0:T(8,128)(2,1)S(1)} %copy-done, bf16[16,512]{1,0:T(8,128)(2,1)S(1)} %copy-done.1), custom_call_target="tpu_custom_call" | custom-call | flops 800000000 | bytes 1000000 | tf_op jit(solution)/shard_map/outer_rows/pallas_call | solution.py:413
  23.2 0.0 collective-permute-done.2.ha_ref
  23.2 0.0 collective-permute-done.3.hb_ref
  23.2 3.2 %closing.1 = (f32[16,64,128]{2,1,0:T(8,128)}, f32[64,128]{1,0:T(8,128)}, f32[64,128]{1,0:T(8,128)}) custom-call(f32[80,128]{1,0:T(8,128)S(1)} %get-tuple-element.29.qa_ref, f32[80,128]{1,0:T(8,128)S(1)} %get-tuple-element.30.qb_ref, f32[80,128]{1,0:T(8,128)S(1)} %collective-permute-done.2.ha_ref, f32[80,128]{1,0:T(8,128)S(1)} %collective-permute-done.3.hb_ref, ...), custom_call_target="tpu_custom_call" | custom-call | flops 100000000 | bytes 3000000 | tf_op jit(solution)/shard_map/closing/pallas_call | solution.py:415
Async XLA Ops:
  0.6 6.8 %copy-start.2 = (bf16[9,128,16]{1,2,0:T(8,128)(2,1)S(1)}, bf16[9,128,16]{1,2,0:T(8,128)(2,1)}, u32[]{:S(2)}) copy-start(bf16[9,128,16]{1,2,0:T(8,128)(2,1)} %param.15) | copy-start | bytes 110596
  3.6 7.4 %collective-permute-start = (f32[88,128]{1,0:T(8,128)S(1)}, f32[88,128]{1,0:T(8,128)S(1)}, u32[]{:S(2)}, u32[]{:S(2)}) collective-permute-start(f32[88,128]{1,0:T(8,128)S(1)} %get-tuple-element.20), channel_id=1, source_target_pairs={{0,1},{1,0},{2,3},{3,2},{4,5},{5,4},{6,7},{7,6},{8,9},{9,8},{10,11... | collective-permute-start | bytes 135176 | tf_op jit(solution)/shard_map/ppermute | solution.py:390
  5.3 2.4 %copy-start = (bf16[512,128]{1,0:T(8,128)(2,1)S(1)}, bf16[512,128]{1,0:T(8,128)(2,1)}, u32[]{:S(2)}) copy-start(bf16[512,128]{1,0:T(8,128)(2,1)} %w2_ref.5) | copy-start | bytes 393220
  5.3 2.4 %copy-start.1 = (bf16[16,512]{1,0:T(8,128)(2,1)S(1)}, bf16[16,512]{1,0:T(8,128)(2,1)}, u32[]{:S(2)}) copy-start(bf16[16,512]{1,0:T(8,128)(2,1)} %w3_ref.5) | copy-start | bytes 49156
  5.3 7.7 %collective-permute-start.1 = (f32[88,128]{1,0:T(8,128)S(1)}, f32[88,128]{1,0:T(8,128)S(1)}, u32[]{:S(2)}, u32[]{:S(2)}) collective-permute-start(f32[88,128]{1,0:T(8,128)S(1)} %get-tuple-element.21), channel_id=1, source_target_pairs={{0,8},{1,2},{2,1},{3,4},{4,3},{5,6},{6,5},{7,255},{8,0},{9,10},{10... | collective-permute-start | bytes 135176 | tf_op jit(solution)/shard_map/ppermute | solution.py:390
  13.2 10.0 %collective-permute-start.2 = (f32[80,128]{1,0:T(8,128)S(1)}, f32[80,128]{1,0:T(8,128)S(1)}, u32[]{:S(2)}, u32[]{:S(2)}) collective-permute-start(f32[80,128]{1,0:T(8,128)S(1)} %get-tuple-element.29.qa_ref), channel_id=1, source_target_pairs={{0,8},{1,9},{2,10},{3,11},{4,12},{5,13},{6,14},{7,15},{8,0},{9,1},... | collective-permute-start | bytes 122888 | tf_op jit(solution)/shard_map/ppermute | solution.py:390
  13.3 9.9 %collective-permute-start.3 = (f32[80,128]{1,0:T(8,128)S(1)}, f32[80,128]{1,0:T(8,128)S(1)}, u32[]{:S(2)}, u32[]{:S(2)}) collective-permute-start(f32[80,128]{1,0:T(8,128)S(1)} %get-tuple-element.30.qb_ref), channel_id=1, source_target_pairs={{0,248},{1,249},{2,250},{3,251},{4,252},{5,253},{6,254},{7,255},{8... | collective-permute-start | bytes 122888 | tf_op jit(solution)/shard_map/ppermute | solution.py:390

commit v2 on v1

--- a/solution.py
+++ b/solution.py
@@ -1,3 +1,5 @@
+import functools
+
 import jax
 import jax.numpy as jnp
 from jax import lax
@@ -10,6 +12,7 @@
 BF16 = jnp.bfloat16
 C0 = 0.7978845608028654
 C1 = 0.044715 * C0
+DRY = 1e30
 VM = pl.BlockSpec(memory_space=pltpu.VMEM)
 HB = pl.BlockSpec(memory_space=pltpu.HBM)
 NT = (((1,), (1,)), ((), ()))
@@ -51,8 +54,8 @@
 
 
 def inside(t_hbm, l_hbm, d_hbm, now_hbm, prior_hbm, mix_hbm,
-           warm_ref, wet_ref, fk_ref, fc_ref, rt_ref, rf_ref, own_ref, np_ref, mx_ref, pa_ref, pb_ref,
-           t_ref, l_ref, d_ref, mix_ref, sems):
+           t_ref, warm_ref, wet_ref, fk_ref, fc_ref, own_ref, np_ref, mx_ref, pa_ref, pb_ref,
+           l_ref, d_ref, mix_ref, q_ref, sems):
     lat = lax.axis_index("lat")
     copies = [pltpu.make_async_copy(d_hbm, d_ref, sems.at[0]), pltpu.make_async_copy(mix_hbm, mix_ref, sems.at[1])]
     for c in range(4):
@@ -63,44 +66,41 @@
     copies.append(pltpu.make_async_copy(prior_hbm, np_ref.at[1], sems.at[11]))
     for copy in copies:
         copy.start()
+    dims = (64, 128)
+    lane = iota(dims, 1)
+    q_ref[:, 0:8, :] = jnp.full((16, 8, 128), DRY, F32)
+    q_ref[:, 72:80, :] = jnp.full((16, 8, 128), DRY, F32)
+    column = jnp.zeros(dims, F32)
+    forcing = jnp.zeros(dims, F32)
     copies[0].wait()
     copies[1].wait()
-    dims = (64, 128)
-    lane, row = iota(dims, 1), iota(dims, 0)
     depth = d_ref[...]
-    column = jnp.zeros(dims, F32)
-    forcing = jnp.zeros(dims, F32)
-    rt = jnp.zeros(dims, F32)
-    rf = jnp.zeros(dims, F32)
-
-    def around(x):
-        east = jnp.where(lane == 127, 0.0, roll(x, 127, 1))
-        west = jnp.where(lane == 0, 0.0, roll(x, 1, 1))
-        north = jnp.where(row == 63, 0.0, roll(x, 63, 0))
-        south = jnp.where(row == 0, 0.0, roll(x, 1, 0))
-        return (east + west) + (north + south)
-
     for k in range(16):
         if k % 4 == 0:
             copies[2 + k // 2].wait()
             copies[3 + k // 2].wait()
         t = t_ref[k]
-        wet = jnp.where(k < depth, l_ref[k].astype(F32), 0.0)
+        water = (l_ref[k] > 0) & (k < depth)
+        q = jnp.where(water, t, DRY)
+        q_ref[k, 8:72, :] = q
+        wet = jnp.where(water, 1.0, 0.0).astype(F32)
         wet_ref[k] = wet
-        warm = t + (mix_ref[k] * wet) * (around(wet * t) - t * around(wet))
-        feature = wet * warm
+
+        def term(n):
+            return jnp.where(n < DRY, n - t, 0.0)
+
+        east = jnp.where(lane == 127, DRY, roll(q, 127, 1))
+        west = jnp.where(lane == 0, DRY, roll(q, 1, 1))
+        inflow = (term(q_ref[k, 7:71, :]) + term(q_ref[k, 9:73, :])) + (term(west) + term(east))
+        warm = t + mix_ref[k] * jnp.where(water, inflow, 0.0)
+        feature = jnp.where(water, warm, 0.0)
         warm_ref[k] = warm
         fk_ref[pl.ds(k, 64, stride=16), :] = feature
         column = column + wet
         forcing = forcing + feature
-        rt = jnp.where(lane >> 1 == k, roll(t, 2 * k + 1, 1), rt)
-        rt = jnp.where(lane >> 1 == 16 + k, roll(wet, 33 + 2 * k, 1), rt)
-        rf = jnp.where(lane >> 3 == k, roll(feature, 8 * k + 4, 1), rf)
     forcing = 0.01 * forcing
     fc_ref[0] = forcing
     fc_ref[1] = column
-    rt_ref[...] = rt
-    rf_ref[...] = rf
 
     copies[10].wait()
     copies[11].wait()
@@ -113,8 +113,8 @@
     def payload(r, first):
         own = jnp.concatenate([t_ref[:, r, :], wet_ref[:, r, :]], axis=0)
         feature = fk_ref[16 * r : 16 * r + 16, :]
-        rows = [x[first : first + 8] for x in (forcing, column, np_ref[0], np_ref[1], rt)]
-        return own, jnp.concatenate([own, feature] + rows, axis=0)
+        rows = [x[first : first + 8] for x in (forcing, column, np_ref[0], np_ref[1])]
+        return own, jnp.concatenate([own, feature] + rows + [edge_pairs(t_ref, wet_ref, first)], axis=0)
 
     own_low, low = payload(0, 0)
     own_high, high = payload(63, 56)
@@ -136,6 +136,23 @@
             pb_ref[8 * i : 8 * i + 8, :] = x
 
 
+def edge_pairs(t_ref, wet_ref, first):
+    pair = iota((8, 128), 1) >> 1
+    rt = jnp.zeros((8, 128), F32)
+    for k in range(16):
+        rt = jnp.where(pair == k, roll(t_ref[k, first : first + 8, :], 2 * k + 1, 1), rt)
+        rt = jnp.where(pair == 16 + k, roll(wet_ref[k, first : first + 8, :], 33 + 2 * k, 1), rt)
+    return rt
+
+
+def edge_features(fk_ref, first):
+    part = iota((8, 128), 1) >> 3
+    rf = jnp.zeros((8, 128), F32)
+    for k in range(16):
+        rf = jnp.where(part == k, roll(fk_ref[pl.ds(16 * first + k, 8, stride=16), :], 8 * k + 4, 1), rf)
+    return rf
+
+
 def between(pa_ref, pb_ref, own_ref, fk_ref, fc_ref, rt_ref, rf_ref, np_ref, mx_ref,
             e4_ref, fb_ref, dd_ref, rfx_ref, qa_ref, qb_ref):
     lat = lax.axis_index("lat")
@@ -204,14 +221,6 @@
     qb_ref[...] = jnp.where(first_core, q_west, q_east)
 
 
-def stencil(w1_ref):
-    return jnp.concatenate([w1_ref[3 * a + b] for b in range(3) for a in range(3)], axis=1)
-
-
-def halves(w2_ref, w3_ref):
-    return (w2_ref[...].astype(F32) * 0.5).astype(BF16), (w3_ref[...].astype(F32) * 0.5).astype(BF16)
-
-
 def layers(w1, w2, w3, window):
     h = gelu_twice(jnp.dot(w1, window, preferred_element_type=F32)).astype(BF16)
     y = gelu_twice(jnp.dot(w2, h, preferred_element_type=F32)).astype(BF16)
@@ -219,47 +228,82 @@
     return 0.5 * net.astype(BF16).astype(F32)
 
 
-GROUP = 16
-
-
-def sweep(w1_ref, w2_ref, w3_ref, g_ref, fw, f0, fe, starts):
-    w1 = stencil(w1_ref)
-    w2, w3 = halves(w2_ref, w3_ref)
-    for g in range(0, len(starts), GROUP):
-        windows = [
-            jnp.concatenate([f[16 * at : 16 * at + 48, :] for f in (fw, f0, fe)], axis=0)
-            for at in starts[g : g + GROUP]
-        ]
-        net = layers(w1, w2, w3, jnp.concatenate(windows, axis=1))
-        for i in range(GROUP):
-            g_ref[16 * (g + i) : 16 * (g + i) + 16, :] = net[:, 128 * i : 128 * i + 128]
-
-
-def put(fw, f0, fe, at, x):
+def put(planes, at, x):
     n = x.shape[0]
-    f0[at : at + n, :] = x.astype(BF16)
-    fw[at : at + n, :] = roll(x, 1, 1).astype(BF16)
-    fe[at : at + n, :] = roll(x, 127, 1).astype(BF16)
-
-
-def middle_rows(fk_ref, w1_ref, w2_ref, w3_ref, g_ref, fw, f0, fe):
-    put(fw, f0, fe, 0, fk_ref[16 * 7 : 16 * 41, :])
-    sweep(w1_ref, w2_ref, w3_ref, g_ref, fw, f0, fe, list(range(32)))
-
-
-def outer_rows(fk_ref, fb_ref, w1_ref, w2_ref, w3_ref, g_ref, fw, f0, fe):
-    put(fw, f0, fe, 0, fk_ref[16 * 39 : 16 * 63, :])
-    put(fw, f0, fe, 16 * 24, fb_ref[32:64, :])
-    put(fw, f0, fe, 16 * 26, fb_ref[0:32, :])
-    put(fw, f0, fe, 16 * 28, fk_ref[16 : 16 * 9, :])
-    sweep(w1_ref, w2_ref, w3_ref, g_ref, fw, f0, fe, [i + 2 * (i >= 24) for i in range(32)])
+    for plane, shift in zip(planes, (1, 0, 127)):
+        plane[at : at + n, :] = roll(x, shift, 1).astype(BF16)
+
+
+def chunk(weights, planes, starts, g_ref, at):
+    w1, w2, w3 = (w[...] for w in weights)
+    windows = [jnp.concatenate([f[16 * r : 16 * r + 48, :] for f in planes], axis=0) for r in starts]
+    net = layers(w1, w2, w3, jnp.concatenate(windows, axis=1))
+    for i in range(16):
+        g_ref[16 * (at + i) : 16 * (at + i) + 16, :] = net[:, 128 * i : 128 * i + 128]
+
+
+def inner_chunk(fk_ref, weights, planes, c, g_ref, at):
+    put(planes, 0, fk_ref[16 * (7 + 16 * c) : 16 * (25 + 16 * c), :])
+    chunk(weights, planes, range(16), g_ref, at)
+
+
+def early_rows():
+    lon, lat = lax.axis_index("lon"), lax.axis_index("lat")
+    place = (lon % 16) // 2
+    return (lat == 7) & (place <= 2), (lat == 7) & (place <= 1)
+
+
+def late_rows():
+    return lax.axis_index("lon") % 16 >= 14
+
+
+def ahead(fk_ref, w1_ref, w2_ref, w3_ref, w1_out, w2_out, w3_out, g_ref, *planes):
+    w1_out[...] = jnp.concatenate([w1_ref[3 * a + b] for b in range(3) for a in range(3)], axis=1)
+    w2_out[...] = (w2_ref[...].astype(F32) * 0.5).astype(BF16)
+    w3_out[...] = (w3_ref[...].astype(F32) * 0.5).astype(BF16)
+    weights = (w1_out, w2_out, w3_out)
+    for c, early in enumerate(early_rows()):
+        pl.when(early)(functools.partial(inner_chunk, fk_ref, weights, planes, c, g_ref, 16 * c))
+
+
+def middle_rows(fk_ref, t_ref, wet_ref, w1_ref, w2_ref, w3_ref, done_ref, g_ref, rt_ref, rf_ref, *planes):
+    weights = (w1_ref, w2_ref, w3_ref)
+    for c, early in enumerate(early_rows()):
+        skip = early | late_rows() if c else early
+        pl.when(jnp.logical_not(skip))(functools.partial(inner_chunk, fk_ref, weights, planes, c, g_ref, 16 * c))
+
+        def take(c=c):
+            g_ref[256 * c : 256 * c + 256, :] = done_ref[256 * c : 256 * c + 256, :]
+
+        pl.when(early)(take)
+    for i in range(0, 64, 8):
+        rt_ref[i : i + 8, :] = edge_pairs(t_ref, wet_ref, i)
+        rf_ref[i : i + 8, :] = edge_features(fk_ref, i)
+    inner_chunk(fk_ref, weights, planes, 2, g_ref, 32)
+
+
+def outer_rows(fk_ref, fb_ref, w1_ref, w2_ref, w3_ref, g1_ref, g_ref, *planes):
+    weights = (w1_ref, w2_ref, w3_ref)
+    late = late_rows()
+    pl.when(late)(functools.partial(inner_chunk, fk_ref, weights, planes, 1, g_ref, 16))
+
+    @pl.when(jnp.logical_not(late))
+    def _():
+        g_ref[256:512, :] = g1_ref[256:512, :]
+
+    put(planes, 0, fb_ref[0:32, :])
+    put(planes, 16 * 2, fk_ref[16 : 16 * 9, :])
+    put(planes, 16 * 10, fk_ref[16 * 55 : 16 * 63, :])
+    put(planes, 16 * 18, fb_ref[32:64, :])
+    chunk(weights, planes, [r + 2 * (r >= 8) for r in range(16)], g_ref, 0)
 
 
 def closing(qa_ref, qb_ref, ha_ref, hb_ref, rf_ref, e4_ref, dd_ref, warm_ref, wet_ref,
-            g1_ref, g2_ref, w1_ref, w2_ref, w3_ref, mx_ref, out_hbm, eta_ref, mid_ref, out_ref, sems):
+            g1_ref, g2_ref, w1_ref, w2_ref, w3_ref, mx_ref, out_hbm, eta_hbm, mid_hbm, out_ref, eta_ref, sems):
     first_core = lax.axis_index("lon") % 2 == 0
     ext = (80, 128)
-    lane, row = iota(ext, 1), iota(ext, 0)
+    lane = iota(ext, 1)
+    small, sub = iota((8, 128), 1), iota((8, 128), 0)
     qa, qb, ha, hb = qa_ref[...], qb_ref[...], ha_ref[...], hb_ref[...]
     q_west, q_east = jnp.where(first_core, qb, qa), jnp.where(first_core, qa, qb)
     h_west, h_east = jnp.where(first_core, hb, ha), jnp.where(first_core, ha, hb)
@@ -269,6 +313,24 @@
         return mix * roll(halo * own, 112, 1) * (halo - own)
 
     d_west, d_east = delta(h_west, q_west), delta(h_east, q_east)
+
+    rf = rf_ref[...]
+    index_w = jnp.where(small < 64, 8 * (small & 15) + 3 + (small >> 4), 0)
+    index_e = jnp.where(small < 64, 8 * (small & 15) + 1 + (small >> 4), 0)
+    f_west = jnp.concatenate([lanes_from(rf[8 * i : 8 * i + 8], index_w) for i in range(10)], axis=0)
+    f_east = jnp.concatenate([lanes_from(rf[8 * i : 8 * i + 8], index_e) for i in range(10)], axis=0)
+    which = lane >> 4
+    f_west = jnp.where(which == 0, roll(h_west, 96, 1) - d_west,
+                       f_west + jnp.where(which == 1, roll(d_west, 16, 1), 0.0))
+    f_east = jnp.where(which == 3, roll(h_east, 16, 1) - roll(d_east, 48, 1),
+                       f_east + jnp.where(which == 2, roll(d_east, 32, 1), 0.0))
+    cells = [f_east, roll(f_east, 112, 1), f_west, roll(f_west, 112, 1)]
+    blank = jnp.zeros((128, 80), BF16)
+    x = jnp.zeros((256, 128), F32)
+    for a in range(3):
+        window = jnp.concatenate([c[7 + a : 71 + a] for c in cells], axis=0).astype(BF16)
+        w = jnp.concatenate([w1_ref[3 * a + b] for b in range(3)] + [blank], axis=1)
+        x = x + lax.dot_general(window, w, NT, preferred_element_type=F32)
 
     side = []
     for i in range(4):
@@ -281,8 +343,6 @@
     push = [main[0] + jnp.where(lane == 0, s_west, 0.0) + jnp.where(lane == 127, s_east, 0.0),
             side[0] - jnp.where(lane == 127, s_west, 0.0) - jnp.where(lane == 0, s_east, 0.0)]
     speed = [0.45 * x / 16 for x in (main[1], side[1])]
-    current = [main[2], side[2]]
-    earlier = [main[3], side[3]]
 
     def neighbours(pair):
         out = []
@@ -295,7 +355,8 @@
 
     active = [jnp.where(s > 0.0, 1.0, 0.0).astype(F32) for s in speed]
     facing = [[jnp.minimum(s, n) for n in ns] for s, ns in zip(speed, neighbours(speed))]
-    for _ in range(SUB):
+
+    def advance(current, earlier):
         fresh = []
         for i, ns in enumerate(neighbours(current)):
             c = current[i]
@@ -303,33 +364,26 @@
             for f, n in zip(facing[i], ns):
                 change = change + f * (n - c)
             fresh.append(active[i] * change)
-        current, earlier = fresh, current
-    eta_ref[...] = current[0][8:72]
-    mid_ref[...] = earlier[0][8:72]
-
-    small = iota((8, 128), 1)
-    rf = rf_ref[...]
-    index_w = jnp.where(small < 64, 8 * (small & 15) + 3 + (small >> 4), 0)
-    index_e = jnp.where(small < 64, 8 * (small & 15) + 1 + (small >> 4), 0)
-    f_west = jnp.concatenate([lanes_from(rf[8 * i : 8 * i + 8], index_w) for i in range(10)], axis=0)
-    f_east = jnp.concatenate([lanes_from(rf[8 * i : 8 * i + 8], index_e) for i in range(10)], axis=0)
-    which = lane >> 4
-    f_west = jnp.where(which == 0, roll(h_west, 96, 1) - d_west,
-                       f_west + jnp.where(which == 1, roll(d_west, 16, 1), 0.0))
-    f_east = jnp.where(which == 3, roll(h_east, 16, 1) - roll(d_east, 48, 1),
-                       f_east + jnp.where(which == 2, roll(d_east, 32, 1), 0.0))
-    cells = [f_east, roll(f_east, 112, 1), f_west, roll(f_west, 112, 1)]
-    w2, w3 = halves(w2_ref, w3_ref)
-    blank = jnp.zeros((128, 80), BF16)
-    x = jnp.zeros((256, 128), F32)
-    for a in range(3):
-        window = jnp.concatenate([c[7 + a : 71 + a] for c in cells], axis=0).astype(BF16)
-        w = jnp.concatenate([w1_ref[3 * a + b] for b in range(3)] + [blank], axis=1)
-        x = x + lax.dot_general(window, w, NT, preferred_element_type=F32)
+        return fresh, current
+
+    state = ([main[2], side[2]], [main[3], side[3]])
+
     h = gelu_twice(x).astype(BF16)
-    y = gelu_twice(lax.dot_general(h, w2, NT, preferred_element_type=F32)).astype(BF16)
-    w3 = jnp.concatenate([w3, jnp.zeros((112, 512), BF16)], axis=0)
+    x = lax.dot_general(h, w2_ref[...], NT, preferred_element_type=F32)
+    state = advance(*state)
+    state = advance(*state)
+    y = gelu_twice(x).astype(BF16)
+    w3 = jnp.concatenate([w3_ref[...], jnp.zeros((112, 512), BF16)], axis=0)
     net = lax.dot_general(y, w3, NT, preferred_element_type=F32)
+    for _ in range(SUB - 2):
+        state = advance(*state)
+    eta_ref[0] = state[0][0][8:72]
+    eta_ref[1] = state[1][0][8:72]
+    copies = [pltpu.make_async_copy(eta_ref.at[0], eta_hbm, sems.at[4]),
+              pltpu.make_async_copy(eta_ref.at[1], mid_hbm, sems.at[5])]
+    copies[0].start()
+    copies[1].start()
+
     net = 0.5 * net.astype(BF16).astype(F32)
     ends = [net[64 * c : 64 * c + 64] for c in range(4)]
     low16 = lane[:64] < 16
@@ -344,16 +398,14 @@
         edges.append(x)
 
     at_edge = (small < 2) | (small >= 126)
-    sub = iota((8, 128), 0)
-    copies = []
     for k in range(16):
         for i in range(8):
-            if i == 0:
-                g = g2_ref[pl.ds(24 * 16 + k, 8, stride=16), :]
-            elif i < 5:
+            if i == 0 or i == 7:
+                g = g2_ref[pl.ds((0 if i == 0 else 128) + k, 8, stride=16), :]
+            elif i == 3 or i == 4:
+                g = g2_ref[pl.ds((8 * i - 8) * 16 + k, 8, stride=16), :]
+            else:
                 g = g1_ref[pl.ds((8 * i - 8) * 16 + k, 8, stride=16), :]
-            else:
-                g = g2_ref[pl.ds((8 * i - 40) * 16 + k, 8, stride=16), :]
             g = jnp.where(at_edge, roll(edges[i], 126 - 4 * k, 1), g)
             y = warm_ref[k, 8 * i : 8 * i + 8, :] + wet_ref[k, 8 * i : 8 * i + 8, :] * g
             if i == 0:
@@ -391,33 +443,41 @@
 
 
 def on_device(t, now, prior, liquid, depth, mix, w1, w2, w3):
-    cube, flat, tall = (16, 64, 128), (64, 128), (80, 128)
-    warm, wet, fk, fc, rt, rf, own, both, mx, pa, pb = call(
+    cube, flat, tall, inner = (16, 64, 128), (64, 128), (80, 128), (768, 128)
+    tv, warm, wet, fk, fc, own, both, mx, pa, pb = call(
         inside,
-        (shape(*cube), shape(*cube), shape(1024, 128), shape(2, 64, 128), shape(*flat), shape(*flat),
+        (shape(*cube), shape(*cube), shape(*cube), shape(1024, 128), shape(2, 64, 128),
          shape(*flat), shape(2, 64, 128), shape(24, 128), shape(88, 128), shape(88, 128)),
-        scratch=(pltpu.VMEM(cube, F32), pltpu.VMEM(cube, jnp.int32), pltpu.VMEM(flat, jnp.int32),
-                 pltpu.SMEM((16,), F32), pltpu.SemaphoreType.DMA((12,))),
+        scratch=(pltpu.VMEM(cube, jnp.int32), pltpu.VMEM(flat, jnp.int32), pltpu.SMEM((16,), F32),
+                 pltpu.VMEM((16, 80, 128), F32), pltpu.SemaphoreType.DMA((12,))),
         specs=[HB] * 6, name="inside", flops=10**7, moved=2 * 10**6,
     )(*(pltpu.with_memory_space_constraint(x, pltpu.HBM) for x in (t, liquid, depth, now, prior, mix)))
-    ra, rb = swap(pa, LAT_A), swap(pb, LAT_B)
-    plane = [pltpu.VMEM((36 * 16, 128), BF16)] * 3
-    g1 = call(middle_rows, shape(512, 128), scratch=plane, specs=[VM] * 4, name="middle_rows",
-              flops=8 * 10**8, moved=10**6)(fk, w1, w2, w3)
+    planes = [pltpu.VMEM((20 * 16, 128), BF16)] * 3
+    ra = swap(pa, LAT_A)
+    v1, v2, v3, gp = call(
+        ahead, (shape(128, 144, dtype=BF16), shape(512, 128, dtype=BF16), shape(16, 512, dtype=BF16), shape(512, 128)),
+        scratch=planes, specs=[VM] * 4, name="ahead", flops=10**6, moved=10**5,
+    )(fk, w1, w2, w3)
+    pb, gp = lax.optimization_barrier((pb, gp))
+    rb = swap(pb, LAT_B)
+    g1, rt, rf = call(middle_rows, (shape(*inner), shape(*flat), shape(*flat)), scratch=planes,
+                      specs=[VM] * 7, name="middle_rows", flops=10**9, moved=10**6,
+                      )(fk, tv, wet, v1, v2, v3, gp)
     e4, fb, dd, rfx, qa, qb = call(
         between,
         (shape(4, 80, 128), shape(64, 128), shape(32, 128), shape(*tall), shape(*tall), shape(*tall)),
         specs=[VM] * 9, name="between", flops=10**7, moved=10**6,
     )(ra, rb, own, fk, fc, rt, rf, both, mx)
-    ha, hb = swap(qa, LON_A), swap(qb, LON_B)
-    g2 = call(outer_rows, shape(512, 128), scratch=plane, specs=[VM] * 5, name="outer_rows",
-              flops=8 * 10**8, moved=10**6)(fk, fb, w1, w2, w3)
+    hb = swap(qb, LON_B)
+    ha = swap(qa, LON_A)
+    g2 = call(outer_rows, shape(512, 128), scratch=planes, specs=[VM] * 6, name="outer_rows",
+              flops=5 * 10**8, moved=10**6)(fk, fb, v1, v2, v3, g1)
     return call(
         closing,
         (shape(*cube), shape(*flat), shape(*flat)),
-        scratch=(pltpu.VMEM(cube, F32), pltpu.SemaphoreType.DMA((4,))),
-        specs=[VM] * 15, out_specs=(HB, VM, VM), name="closing", flops=10**8, moved=3 * 10**6,
-    )(qa, qb, ha, hb, rfx, e4, dd, warm, wet, g1, g2, w1, w2, w3, mx)
+        scratch=(pltpu.VMEM(cube, F32), pltpu.VMEM((2, 64, 128), F32), pltpu.SemaphoreType.DMA((6,))),
+        specs=[VM] * 15, out_specs=(HB, HB, HB), name="closing", flops=10**8, moved=3 * 10**6,
+    )(qa, qb, ha, hb, rfx, e4, dd, warm, wet, g1, g2, w1, v2, v3, mx)
 
 
 def solution(mesh):

time: 26.5 us -> 24 us (0.906)
  waiting for transfers between devices: 1.99 us -> 0.11 us
  Pallas kernels: 13 us -> 12.1 us
    ppermute x4, waiting for transfers between devices: 1.99 us -> 0.11 us  [swap(): return lax.ppermute(x, ('lon', 'lat'), pairs)]
    pallas_call x1, Pallas kernels: 3.22 us -> 2.51 us  [on_device(): call(closing, (shape(*cube), shape(*flat), shape(*flat)), scratch=(pltpu....]
    pallas_call x3 -> x4, Pallas kernels: 9.58 us -> 9.38 us  [the longest x1 5.42 us: on_device(): call(middle_rows, (shape(*inner), shape(*flat), shape(*flat)), scratch=pl...]
  transfers between devices with their start and end apart: 4 -> 4, of which waited for: 1 -> 1; matrix products, arithmetic and copies ran while one was open for 1% -> 1% of each run, Pallas kernels for 25% -> 31%
where the time goes in v2:
time: 24 us; the launch traced here: 23.9 us
  Pallas kernels  12.1 us (50%)
  starting transfers between devices  10.6 us (44%)
  between operations  0.89 us (4%)
  local copies, waits for them, and re-layouts  0.24 us (1%)
    ppermute x4, starting transfers between devices, swap(): return lax.ppermute(x, ('lon', 'lat'), pairs)  10.6 us
    pallas_call x1, Pallas kernels, on_device(): call(middle_rows, (shape(*inner), shape(*flat), shape(*flat)), scratch=pl...  5.42 us
    pallas_call x1, Pallas kernels, on_device(): call(closing, (shape(*cube), shape(*flat), shape(*flat)), scratch=(pltpu....  2.51 us
    pallas_call x1, Pallas kernels, on_device(): call(inside, (shape(*cube), shape(*cube), shape(*cube), shape(1024, 128),...  2.05 us
    pallas_call x1, Pallas kernels, on_device(): call(outer_rows, shape(512, 128), scratch=planes, specs=[VM] * 6, name='o...  1.77 us
  transfers between devices with their start and end apart: 4, of which 1 were waited for; matrix products, arithmetic and copies ran while one was open for 1% of the time, Pallas kernels for 31%

profile of v2, /device:TPU:4, one launch (start us, length us, event | category | flops | bytes accessed | tf_op | source)
XLA Modules:
  0.0 23.9 jit_solution(7219524384258088193)
XLA Ops:
  0.6 0.0 copy-start.2
  0.6 2.0 %inside.1 = (f32[16,64,128]{2,1,0:T(8,128)S(1)}, f32[16,64,128]{2,1,0:T(8,128)S(1)}, f32[16,64,128]{2,1,0:T(8,128)S(1)}, f32[1024,128]{1,0:T(8,128)S(1)}, f32[2,...) custom-call(f32[16,64,128]{2,1,0:T(8,128)} %t_hbm.1, ...), custom_call_target="tpu_custom_call" | custom-call | flops 10000000 | bytes 2000000 | tf_op jit(solution)/shard_map/inside/pallas_call | solution.py:447
  2.7 0.0 copy-start
  2.7 0.0 copy-start.1
  2.7 1.7 %collective-permute-start = (f32[88,128]{1,0:T(8,128)S(1)}, f32[88,128]{1,0:T(8,128)S(1)}, u32[]{:S(2)}, u32[]{:S(2)}) collective-permute-start(f32[88,128]{1,0:T(8,128)S(1)} %get-tuple-element.28), channel_id=1, source_target_pairs={{0,1},{1,0},{2,3},{3,2},{4,5},{5,4},{6,7},{7,6},{8,9},{9,8},{10,11... | collective-permute-start | bytes 135176 | tf_op jit(solution)/shard_map/ppermute | solution.py:442
  4.4 0.0 copy-done.2
  4.4 0.2 copy.12.w1_ref
  4.6 0.0 copy-done
  4.6 0.0 copy-done.1
  4.6 0.1 ahead.1
  4.8 2.2 %collective-permute-start.1 = (f32[88,128]{1,0:T(8,128)S(1)}, f32[88,128]{1,0:T(8,128)S(1)}, u32[]{:S(2)}, u32[]{:S(2)}) collective-permute-start(f32[88,128]{1,0:T(8,128)S(1)} %get-tuple-element.32), channel_id=1, source_target_pairs={{0,8},{1,2},{2,1},{3,4},{4,3},{5,6},{6,5},{7,255},{8,0},{9,10},{10... | collective-permute-start | bytes 135176 | tf_op jit(solution)/shard_map/ppermute | solution.py:442
  7.0 5.4 %middle_rows.1 = (f32[768,128]{1,0:T(8,128)S(1)}, f32[64,128]{1,0:T(8,128)S(1)}, f32[64,128]{1,0:T(8,128)S(1)}) custom-call(f32[1024,128]{1,0:T(8,128)S(1)} %get-tuple-element.30.fk_ref, f32[16,64,128]{2,1,0:T(8,128)S(1)} %get-tuple-element.35.t_ref, f32[16,64,128]{2,1,0:T(8,128)S(1)} %get-tuple-element.36.wet_ref, ...), custom_call_target="tpu_custom_call" | custom-call | flops 1000000000 | bytes 1000000 | tf_op jit(solution)/shard_map/middle_rows/pallas_call | solution.py:463
  12.4 0.0 collective-permute-done.pa_ref
  12.4 0.1 collective-permute-done.1.pb_ref
  12.5 0.2 between.1
  12.8 0.1 collective-permute-start.2
  12.9 6.6 %collective-permute-start.3 = (f32[80,128]{1,0:T(8,128)S(1)}, f32[80,128]{1,0:T(8,128)S(1)}, u32[]{:S(2)}, u32[]{:S(2)}) collective-permute-start(f32[80,128]{1,0:T(8,128)S(1)} %get-tuple-element.46.qb_ref), channel_id=1, source_target_pairs={{0,248},{1,249},{2,250},{3,251},{4,252},{5,253},{6,254},{7,255},{8... | collective-permute-start | bytes 122888 | tf_op jit(solution)/shard_map/ppermute | solution.py:442
  19.4 1.8 %outer_rows.1.g2_ref = f32[512,128]{1,0:T(8,128)S(1)} custom-call(f32[1024,128]{1,0:T(8,128)S(1)} %get-tuple-element.30.fk_ref, f32[64,128]{1,0:T(8,128)S(1)} %get-tuple-element.52.fb_ref, bf16[128,144]{1,0:T(8,128)(2,1)S(1)} %get-tuple-element.37.w1_ref, bf16[512,128]{1,0:T(8,128)(2,1)S(1)} %get-tuple-element.38.w2_ref, ...), custom_call_target="tpu_custom_call" | custom-call | flops 500000000 | bytes 1000000 | tf_op jit(solution)/shard_map/outer_rows/pallas_call | solution.py:473
  21.2 0.0 collective-permute-done.2.ha_ref
  21.2 0.0 collective-permute-done.3.hb_ref
  21.2 2.5 %closing.1 = (f32[16,64,128]{2,1,0:T(8,128)}, f32[64,128]{1,0:T(8,128)}, f32[64,128]{1,0:T(8,128)}) custom-call(f32[80,128]{1,0:T(8,128)S(1)} %get-tuple-element.45.qa_ref, f32[80,128]{1,0:T(8,128)S(1)} %get-tuple-element.46.qb_ref, f32[80,128]{1,0:T(8,128)S(1)} %collective-permute-done.2.ha_ref, f32[80,128]{1,0:T(8,128)S(1)} %collective-permute-done.3.hb_ref, ...), custom_call_target="tpu_custom_call" | custom-call | flops 100000000 | bytes 3000000 | tf_op jit(solution)/shard_map/closing/pallas_call | solution.py:475
Async XLA Ops:
  0.6 3.8 %copy-start.2 = (bf16[9,128,16]{1,2,0:T(8,128)(2,1)S(1)}, bf16[9,128,16]{1,2,0:T(8,128)(2,1)}, u32[]{:S(2)}) copy-start(bf16[9,128,16]{1,2,0:T(8,128)(2,1)} %param.15) | copy-start | bytes 110596
  2.7 1.9 %copy-start = (bf16[512,128]{1,0:T(8,128)(2,1)S(1)}, bf16[512,128]{1,0:T(8,128)(2,1)}, u32[]{:S(2)}) copy-start(bf16[512,128]{1,0:T(8,128)(2,1)} %w2_ref.1) | copy-start | bytes 393220
  2.7 1.9 %copy-start.1 = (bf16[16,512]{1,0:T(8,128)(2,1)S(1)}, bf16[16,512]{1,0:T(8,128)(2,1)}, u32[]{:S(2)}) copy-start(bf16[16,512]{1,0:T(8,128)(2,1)} %w3_ref.1) | copy-start | bytes 49156
  2.7 9.7 %collective-permute-start = (f32[88,128]{1,0:T(8,128)S(1)}, f32[88,128]{1,0:T(8,128)S(1)}, u32[]{:S(2)}, u32[]{:S(2)}) collective-permute-start(f32[88,128]{1,0:T(8,128)S(1)} %get-tuple-element.28), channel_id=1, source_target_pairs={{0,1},{1,0},{2,3},{3,2},{4,5},{5,4},{6,7},{7,6},{8,9},{9,8},{10,11... | collective-permute-start | bytes 135176 | tf_op jit(solution)/shard_map/ppermute | solution.py:442
  4.8 7.7 %collective-permute-start.1 = (f32[88,128]{1,0:T(8,128)S(1)}, f32[88,128]{1,0:T(8,128)S(1)}, u32[]{:S(2)}, u32[]{:S(2)}) collective-permute-start(f32[88,128]{1,0:T(8,128)S(1)} %get-tuple-element.32), channel_id=1, source_target_pairs={{0,8},{1,2},{2,1},{3,4},{4,3},{5,6},{6,5},{7,255},{8,0},{9,10},{10... | collective-permute-start | bytes 135176 | tf_op jit(solution)/shard_map/ppermute | solution.py:442
  12.8 8.5 %collective-permute-start.2 = (f32[80,128]{1,0:T(8,128)S(1)}, f32[80,128]{1,0:T(8,128)S(1)}, u32[]{:S(2)}, u32[]{:S(2)}) collective-permute-start(f32[80,128]{1,0:T(8,128)S(1)} %get-tuple-element.45.qa_ref), channel_id=1, source_target_pairs={{0,8},{1,9},{2,10},{3,11},{4,12},{5,13},{6,14},{7,15},{8,0},{9,1},... | collective-permute-start | bytes 122888 | tf_op jit(solution)/shard_map/ppermute | solution.py:442
  12.9 8.4 %collective-permute-start.3 = (f32[80,128]{1,0:T(8,128)S(1)}, f32[80,128]{1,0:T(8,128)S(1)}, u32[]{:S(2)}, u32[]{:S(2)}) collective-permute-start(f32[80,128]{1,0:T(8,128)S(1)} %get-tuple-element.46.qb_ref), channel_id=1, source_target_pairs={{0,248},{1,249},{2,250},{3,251},{4,252},{5,253},{6,254},{7,255},{8... | collective-permute-start | bytes 122888 | tf_op jit(solution)/shard_map/ppermute | solution.py:442

commit v3 on v2

--- a/solution.py
+++ b/solution.py
@@ -218,7 +218,8 @@
     first_core = lax.axis_index("lon") % 2 == 0
     q_east, q_west = columns(0), columns(1)
     qa_ref[...] = jnp.where(first_core, q_east, q_west)
-    qb_ref[...] = jnp.where(first_core, q_west, q_east)
+    qb_ref[0:80, :] = jnp.where(first_core, q_west, q_east)
+    qb_ref[80:96, :] = jnp.zeros((16, 128), F32)
 
 
 def layers(w1, w2, w3, window):
@@ -250,7 +251,7 @@
 def early_rows():
     lon, lat = lax.axis_index("lon"), lax.axis_index("lat")
     place = (lon % 16) // 2
-    return (lat == 7) & (place <= 2), (lat == 7) & (place <= 1)
+    return (lat == 7) & (place <= 2)
 
 
 def late_rows():
@@ -262,20 +263,19 @@
     w2_out[...] = (w2_ref[...].astype(F32) * 0.5).astype(BF16)
     w3_out[...] = (w3_ref[...].astype(F32) * 0.5).astype(BF16)
     weights = (w1_out, w2_out, w3_out)
-    for c, early in enumerate(early_rows()):
-        pl.when(early)(functools.partial(inner_chunk, fk_ref, weights, planes, c, g_ref, 16 * c))
+    pl.when(early_rows())(functools.partial(inner_chunk, fk_ref, weights, planes, 0, g_ref, 0))
 
 
 def middle_rows(fk_ref, t_ref, wet_ref, w1_ref, w2_ref, w3_ref, done_ref, g_ref, rt_ref, rf_ref, *planes):
     weights = (w1_ref, w2_ref, w3_ref)
-    for c, early in enumerate(early_rows()):
-        skip = early | late_rows() if c else early
-        pl.when(jnp.logical_not(skip))(functools.partial(inner_chunk, fk_ref, weights, planes, c, g_ref, 16 * c))
-
-        def take(c=c):
-            g_ref[256 * c : 256 * c + 256, :] = done_ref[256 * c : 256 * c + 256, :]
-
-        pl.when(early)(take)
+    early = early_rows()
+    pl.when(jnp.logical_not(early))(functools.partial(inner_chunk, fk_ref, weights, planes, 0, g_ref, 0))
+
+    @pl.when(early)
+    def _():
+        g_ref[0:256, :] = done_ref[...]
+
+    pl.when(jnp.logical_not(late_rows()))(functools.partial(inner_chunk, fk_ref, weights, planes, 1, g_ref, 16))
     for i in range(0, 64, 8):
         rt_ref[i : i + 8, :] = edge_pairs(t_ref, wet_ref, i)
         rf_ref[i : i + 8, :] = edge_features(fk_ref, i)
@@ -304,7 +304,7 @@
     ext = (80, 128)
     lane = iota(ext, 1)
     small, sub = iota((8, 128), 1), iota((8, 128), 0)
-    qa, qb, ha, hb = qa_ref[...], qb_ref[...], ha_ref[...], hb_ref[...]
+    qa, qb, ha, hb = qa_ref[...], qb_ref[0:80, :], ha_ref[...], hb_ref[0:80, :]
     q_west, q_east = jnp.where(first_core, qb, qa), jnp.where(first_core, qa, qb)
     h_west, h_east = jnp.where(first_core, hb, ha), jnp.where(first_core, ha, hb)
     mix = mx_ref[16:17, :]
@@ -455,7 +455,7 @@
     planes = [pltpu.VMEM((20 * 16, 128), BF16)] * 3
     ra = swap(pa, LAT_A)
     v1, v2, v3, gp = call(
-        ahead, (shape(128, 144, dtype=BF16), shape(512, 128, dtype=BF16), shape(16, 512, dtype=BF16), shape(512, 128)),
+        ahead, (shape(128, 144, dtype=BF16), shape(512, 128, dtype=BF16), shape(16, 512, dtype=BF16), shape(256, 128)),
         scratch=planes, specs=[VM] * 4, name="ahead", flops=10**6, moved=10**5,
     )(fk, w1, w2, w3)
     pb, gp = lax.optimization_barrier((pb, gp))
@@ -465,7 +465,7 @@
                       )(fk, tv, wet, v1, v2, v3, gp)
     e4, fb, dd, rfx, qa, qb = call(
         between,
-        (shape(4, 80, 128), shape(64, 128), shape(32, 128), shape(*tall), shape(*tall), shape(*tall)),
+        (shape(4, 80, 128), shape(64, 128), shape(32, 128), shape(*tall), shape(*tall), shape(96, 128)),
         specs=[VM] * 9, name="between", flops=10**7, moved=10**6,
     )(ra, rb, own, fk, fc, rt, rf, both, mx)
     hb = swap(qb, LON_B)

time: 24 us -> 22.8 us (0.950)
  the two profiles are of different devices: /device:TPU:4 before, /device:TPU:5 now
where the time goes in v3:
time: 22.8 us; the launch traced here: 22.7 us
  Pallas kernels  12.3 us (54%)
  starting transfers between devices  9.23 us (40%)
  between operations  0.89 us (4%)
  local copies, waits for them, and re-layouts  0.24 us (1%)
    ppermute x4, starting transfers between devices, swap(): return lax.ppermute(x, ('lon', 'lat'), pairs)  9.23 us
    pallas_call x1, Pallas kernels, on_device(): call(middle_rows, (shape(*inner), shape(*flat), shape(*flat)), scratch=pl...  5.43 us
    pallas_call x1, Pallas kernels, on_device(): call(closing, (shape(*cube), shape(*flat), shape(*flat)), scratch=(pltpu....  2.51 us
    pallas_call x1, Pallas kernels, on_device(): call(inside, (shape(*cube), shape(*cube), shape(*cube), shape(1024, 128),...  2.05 us
    pallas_call x1, Pallas kernels, on_device(): call(outer_rows, shape(512, 128), scratch=planes, specs=[VM] * 6, name='o...  1.95 us
  transfers between devices with their start and end apart: 4, of which 0 were waited for; matrix products, arithmetic and copies ran while one was open for 1% of the time, Pallas kernels for 33%

profile of v3, /device:TPU:5, one launch (start us, length us, event | category | flops | bytes accessed | tf_op | source)
XLA Modules:
  0.0 22.7 jit_solution(14759179283115002047)
XLA Ops:
  0.6 0.0 copy-start.2
  0.6 2.0 %inside.1 = (f32[16,64,128]{2,1,0:T(8,128)S(1)}, f32[16,64,128]{2,1,0:T(8,128)S(1)}, f32[16,64,128]{2,1,0:T(8,128)S(1)}, f32[1024,128]{1,0:T(8,128)S(1)}, f32[2,...) custom-call(f32[16,64,128]{2,1,0:T(8,128)} %t_hbm.1, ...), custom_call_target="tpu_custom_call" | custom-call | flops 10000000 | bytes 2000000 | tf_op jit(solution)/shard_map/inside/pallas_call | solution.py:447
  2.7 0.0 copy-start
  2.7 0.0 copy-start.1
  2.7 1.4 %collective-permute-start = (f32[88,128]{1,0:T(8,128)S(1)}, f32[88,128]{1,0:T(8,128)S(1)}, u32[]{:S(2)}, u32[]{:S(2)}) collective-permute-start(f32[88,128]{1,0:T(8,128)S(1)} %get-tuple-element.28), channel_id=1, source_target_pairs={{0,1},{1,0},{2,3},{3,2},{4,5},{5,4},{6,7},{7,6},{8,9},{9,8},{10,11... | collective-permute-start | bytes 135176 | tf_op jit(solution)/shard_map/ppermute | solution.py:442
  4.1 0.0 copy-done.2
  4.1 0.2 copy.12.w1_ref
  4.3 0.0 copy-done
  4.3 0.0 copy-done.1
  4.3 0.1 ahead.1
  4.5 2.0 %collective-permute-start.1 = (f32[88,128]{1,0:T(8,128)S(1)}, f32[88,128]{1,0:T(8,128)S(1)}, u32[]{:S(2)}, u32[]{:S(2)}) collective-permute-start(f32[88,128]{1,0:T(8,128)S(1)} %get-tuple-element.32), channel_id=1, source_target_pairs={{0,8},{1,2},{2,1},{3,4},{4,3},{5,6},{6,5},{7,255},{8,0},{9,10},{10... | collective-permute-start | bytes 135176 | tf_op jit(solution)/shard_map/ppermute | solution.py:442
  6.5 5.4 %middle_rows.1 = (f32[768,128]{1,0:T(8,128)S(1)}, f32[64,128]{1,0:T(8,128)S(1)}, f32[64,128]{1,0:T(8,128)S(1)}) custom-call(f32[1024,128]{1,0:T(8,128)S(1)} %get-tuple-element.30.fk_ref, f32[16,64,128]{2,1,0:T(8,128)S(1)} %get-tuple-element.35.t_ref, f32[16,64,128]{2,1,0:T(8,128)S(1)} %get-tuple-element.36.wet_ref, ...), custom_call_target="tpu_custom_call" | custom-call | flops 1000000000 | bytes 1000000 | tf_op jit(solution)/shard_map/middle_rows/pallas_call | solution.py:463
  11.9 0.0 collective-permute-done.pa_ref
  12.0 0.0 collective-permute-done.1.pb_ref
  12.0 0.2 %between.1 = (f32[4,80,128]{2,1,0:T(8,128)S(1)}, f32[64,128]{1,0:T(8,128)S(1)}, f32[32,128]{1,0:T(8,128)S(1)}, f32[80,128]{1,0:T(8,128)S(1)}, f32[80,128]{1,0:T(8,128)S(1)}, /*index=5*/f32[96,128]{1,0:T(8,128)S(1)}) custom-call(f32[88,128]{1,0:T(8,128)S(1)} %collective-permute-done.pa_ref, f32[88,128]{1,0:T(8,128)S(1)} %collective-permute-done.1.pb_ref, ...), custom_call_target="tpu_custom_call" | custom-call | flops 10000000 | bytes 1000000 | tf_op jit(solution)/shard_map/between/pallas_call | solution.py:466
  12.2 2.8 %collective-permute-start.3 = (f32[96,128]{1,0:T(8,128)S(1)}, f32[96,128]{1,0:T(8,128)S(1)}, u32[]{:S(2)}, u32[]{:S(2)}) collective-permute-start(f32[96,128]{1,0:T(8,128)S(1)} %get-tuple-element.46.qb_ref), channel_id=1, source_target_pairs={{0,248},{1,249},{2,250},{3,251},{4,252},{5,253},{6,254},{7,255},{8... | collective-permute-start | bytes 147464 | tf_op jit(solution)/shard_map/ppermute | solution.py:442
  15.0 3.0 %collective-permute-start.2 = (f32[80,128]{1,0:T(8,128)S(1)}, f32[80,128]{1,0:T(8,128)S(1)}, u32[]{:S(2)}, u32[]{:S(2)}) collective-permute-start(f32[80,128]{1,0:T(8,128)S(1)} %get-tuple-element.45.qa_ref), channel_id=1, source_target_pairs={{0,8},{1,9},{2,10},{3,11},{4,12},{5,13},{6,14},{7,15},{8,0},{9,1},... | collective-permute-start | bytes 122888 | tf_op jit(solution)/shard_map/ppermute | solution.py:442
  18.0 1.9 %outer_rows.1.g2_ref = f32[512,128]{1,0:T(8,128)S(1)} custom-call(f32[1024,128]{1,0:T(8,128)S(1)} %get-tuple-element.30.fk_ref, f32[64,128]{1,0:T(8,128)S(1)} %get-tuple-element.52.fb_ref, bf16[128,144]{1,0:T(8,128)(2,1)S(1)} %get-tuple-element.37.w1_ref, bf16[512,128]{1,0:T(8,128)(2,1)S(1)} %get-tuple-element.38.w2_ref, ...), custom_call_target="tpu_custom_call" | custom-call | flops 500000000 | bytes 1000000 | tf_op jit(solution)/shard_map/outer_rows/pallas_call | solution.py:473
  20.0 0.0 collective-permute-done.2.ha_ref
  20.0 0.0 collective-permute-done.3.hb_ref
  20.0 2.5 %closing.1 = (f32[16,64,128]{2,1,0:T(8,128)}, f32[64,128]{1,0:T(8,128)}, f32[64,128]{1,0:T(8,128)}) custom-call(f32[80,128]{1,0:T(8,128)S(1)} %get-tuple-element.45.qa_ref, f32[96,128]{1,0:T(8,128)S(1)} %get-tuple-element.46.qb_ref, f32[80,128]{1,0:T(8,128)S(1)} %collective-permute-done.2.ha_ref, f32[96,128]{1,0:T(8,128)S(1)} %collective-permute-done.3.hb_ref, ...), custom_call_target="tpu_custom_call" | custom-call | flops 100000000 | bytes 3000000 | tf_op jit(solution)/shard_map/closing/pallas_call | solution.py:475
Async XLA Ops:
  0.6 3.5 %copy-start.2 = (bf16[9,128,16]{1,2,0:T(8,128)(2,1)S(1)}, bf16[9,128,16]{1,2,0:T(8,128)(2,1)}, u32[]{:S(2)}) copy-start(bf16[9,128,16]{1,2,0:T(8,128)(2,1)} %param.15) | copy-start | bytes 110596
  2.7 1.6 %copy-start = (bf16[512,128]{1,0:T(8,128)(2,1)S(1)}, bf16[512,128]{1,0:T(8,128)(2,1)}, u32[]{:S(2)}) copy-start(bf16[512,128]{1,0:T(8,128)(2,1)} %w2_ref.1) | copy-start | bytes 393220
  2.7 1.6 %copy-start.1 = (bf16[16,512]{1,0:T(8,128)(2,1)S(1)}, bf16[16,512]{1,0:T(8,128)(2,1)}, u32[]{:S(2)}) copy-start(bf16[16,512]{1,0:T(8,128)(2,1)} %w3_ref.1) | copy-start | bytes 49156
  2.7 9.2 %collective-permute-start = (f32[88,128]{1,0:T(8,128)S(1)}, f32[88,128]{1,0:T(8,128)S(1)}, u32[]{:S(2)}, u32[]{:S(2)}) collective-permute-start(f32[88,128]{1,0:T(8,128)S(1)} %get-tuple-element.28), channel_id=1, source_target_pairs={{0,1},{1,0},{2,3},{3,2},{4,5},{5,4},{6,7},{7,6},{8,9},{9,8},{10,11... | collective-permute-start | bytes 135176 | tf_op jit(solution)/shard_map/ppermute | solution.py:442
  4.5 7.5 %collective-permute-start.1 = (f32[88,128]{1,0:T(8,128)S(1)}, f32[88,128]{1,0:T(8,128)S(1)}, u32[]{:S(2)}, u32[]{:S(2)}) collective-permute-start(f32[88,128]{1,0:T(8,128)S(1)} %get-tuple-element.32), channel_id=1, source_target_pairs={{0,8},{1,2},{2,1},{3,4},{4,3},{5,6},{6,5},{7,255},{8,0},{9,10},{10... | collective-permute-start | bytes 135176 | tf_op jit(solution)/shard_map/ppermute | solution.py:442
  12.2 7.8 %collective-permute-start.3 = (f32[96,128]{1,0:T(8,128)S(1)}, f32[96,128]{1,0:T(8,128)S(1)}, u32[]{:S(2)}, u32[]{:S(2)}) collective-permute-start(f32[96,128]{1,0:T(8,128)S(1)} %get-tuple-element.46.qb_ref), channel_id=1, source_target_pairs={{0,248},{1,249},{2,250},{3,251},{4,252},{5,253},{6,254},{7,255},{8... | collective-permute-start | bytes 147464 | tf_op jit(solution)/shard_map/ppermute | solution.py:442
  15.0 4.9 %collective-permute-start.2 = (f32[80,128]{1,0:T(8,128)S(1)}, f32[80,128]{1,0:T(8,128)S(1)}, u32[]{:S(2)}, u32[]{:S(2)}) collective-permute-start(f32[80,128]{1,0:T(8,128)S(1)} %get-tuple-element.45.qa_ref), channel_id=1, source_target_pairs={{0,8},{1,9},{2,10},{3,11},{4,12},{5,13},{6,14},{7,15},{8,0},{9,1},... | collective-permute-start | bytes 122888 | tf_op jit(solution)/shard_map/ppermute | solution.py:442

commit v4 on v3

--- a/solution.py
+++ b/solution.py
@@ -245,7 +245,7 @@
 
 def inner_chunk(fk_ref, weights, planes, c, g_ref, at):
     put(planes, 0, fk_ref[16 * (7 + 16 * c) : 16 * (25 + 16 * c), :])
-    chunk(weights, planes, range(16), g_ref, at)
+    chunk(weights, planes, list(range(16)), g_ref, at)
 
 
 def early_rows():
@@ -259,7 +259,8 @@
 
 
 def ahead(fk_ref, w1_ref, w2_ref, w3_ref, w1_out, w2_out, w3_out, g_ref, *planes):
-    w1_out[...] = jnp.concatenate([w1_ref[3 * a + b] for b in range(3) for a in range(3)], axis=1)
+    w1 = jnp.concatenate([w1_ref[3 * a + b] for b in range(3) for a in range(3)], axis=0)
+    w1_out[...] = w1.astype(F32).T.astype(BF16)
     w2_out[...] = (w2_ref[...].astype(F32) * 0.5).astype(BF16)
     w3_out[...] = (w3_ref[...].astype(F32) * 0.5).astype(BF16)
     weights = (w1_out, w2_out, w3_out)
@@ -325,12 +326,12 @@
     f_east = jnp.where(which == 3, roll(h_east, 16, 1) - roll(d_east, 48, 1),
                        f_east + jnp.where(which == 2, roll(d_east, 32, 1), 0.0))
     cells = [f_east, roll(f_east, 112, 1), f_west, roll(f_west, 112, 1)]
-    blank = jnp.zeros((128, 80), BF16)
+    blank = jnp.zeros((80, 128), BF16)
     x = jnp.zeros((256, 128), F32)
     for a in range(3):
         window = jnp.concatenate([c[7 + a : 71 + a] for c in cells], axis=0).astype(BF16)
-        w = jnp.concatenate([w1_ref[3 * a + b] for b in range(3)] + [blank], axis=1)
-        x = x + lax.dot_general(window, w, NT, preferred_element_type=F32)
+        w = jnp.concatenate([w1_ref[3 * a + b] for b in range(3)] + [blank], axis=0)
+        x = x + jnp.dot(window, w, preferred_element_type=F32)
 
     side = []
     for i in range(4):
@@ -443,6 +444,7 @@
 
 
 def on_device(t, now, prior, liquid, depth, mix, w1, w2, w3):
+    w1 = jnp.transpose(w1, (0, 2, 1))
     cube, flat, tall, inner = (16, 64, 128), (64, 128), (80, 128), (768, 128)
     tv, warm, wet, fk, fc, own, both, mx, pa, pb = call(
         inside,

time: 22.8 us -> 22.4 us (0.982)
  local copies, waits for them, and re-layouts: 0.24 us -> 0.01 us
  transfers between devices with their start and end apart: 4 -> 4, of which waited for: 0 -> 0; matrix products, arithmetic and copies ran while one was open for 1% -> 0% of each run, Pallas kernels for 33% -> 33%
where the time goes in v4:
time: 22.4 us; the launch traced here: 22.3 us
  Pallas kernels  12.2 us (54%)
  starting transfers between devices  9.24 us (41%)
  between operations  0.88 us (4%)
    ppermute x4, starting transfers between devices, swap(): return lax.ppermute(x, ('lon', 'lat'), pairs)  9.24 us
    pallas_call x1, Pallas kernels, on_device(): call(middle_rows, (shape(*inner), shape(*flat), shape(*flat)), scratch=pl...  5.4 us
    pallas_call x1, Pallas kernels, on_device(): call(closing, (shape(*cube), shape(*flat), shape(*flat)), scratch=(pltpu....  2.41 us
    pallas_call x1, Pallas kernels, on_device(): call(inside, (shape(*cube), shape(*cube), shape(*cube), shape(1024, 128),...  2.06 us
    pallas_call x1, Pallas kernels, on_device(): call(outer_rows, shape(512, 128), scratch=planes, specs=[VM] * 6, name='o...  1.95 us
  transfers between devices with their start and end apart: 4, of which 0 were waited for; matrix products, arithmetic and copies ran while one was open for 0% of the time, Pallas kernels for 33%

profile of v4, /device:TPU:5, one launch (start us, length us, event | category | flops | bytes accessed | tf_op | source)
XLA Modules:
  0.0 22.3 jit_solution(2990580950944077783)
XLA Ops:
  0.6 0.0 copy-start.1
  0.6 0.0 copy-start
  0.7 0.0 copy-start.2
  0.7 2.1 %inside.1 = (f32[16,64,128]{2,1,0:T(8,128)S(1)}, f32[16,64,128]{2,1,0:T(8,128)S(1)}, f32[16,64,128]{2,1,0:T(8,128)S(1)}, f32[1024,128]{1,0:T(8,128)S(1)}, f32[2,...) custom-call(f32[16,64,128]{2,1,0:T(8,128)} %t_hbm.1, ...), custom_call_target="tpu_custom_call" | custom-call | flops 10000000 | bytes 2000000 | tf_op jit(solution)/shard_map/inside/pallas_call | solution.py:449
  2.7 1.4 %collective-permute-start = (f32[88,128]{1,0:T(8,128)S(1)}, f32[88,128]{1,0:T(8,128)S(1)}, u32[]{:S(2)}, u32[]{:S(2)}) collective-permute-start(f32[88,128]{1,0:T(8,128)S(1)} %get-tuple-element.28), channel_id=1, source_target_pairs={{0,1},{1,0},{2,3},{3,2},{4,5},{5,4},{6,7},{7,6},{8,9},{9,8},{10,11... | collective-permute-start | bytes 135176 | tf_op jit(solution)/shard_map/ppermute | solution.py:443
  4.1 0.0 copy-done.1
  4.1 0.0 copy-done
  4.1 0.0 copy-done.2
  4.1 0.1 ahead.1
  4.2 1.9 %collective-permute-start.1 = (f32[88,128]{1,0:T(8,128)S(1)}, f32[88,128]{1,0:T(8,128)S(1)}, u32[]{:S(2)}, u32[]{:S(2)}) collective-permute-start(f32[88,128]{1,0:T(8,128)S(1)} %get-tuple-element.32), channel_id=1, source_target_pairs={{0,8},{1,2},{2,1},{3,4},{4,3},{5,6},{6,5},{7,255},{8,0},{9,10},{10... | collective-permute-start | bytes 135176 | tf_op jit(solution)/shard_map/ppermute | solution.py:443
  6.2 5.4 %middle_rows.1 = (f32[768,128]{1,0:T(8,128)S(1)}, f32[64,128]{1,0:T(8,128)S(1)}, f32[64,128]{1,0:T(8,128)S(1)}) custom-call(f32[1024,128]{1,0:T(8,128)S(1)} %get-tuple-element.30.fk_ref, f32[16,64,128]{2,1,0:T(8,128)S(1)} %get-tuple-element.35.t_ref, f32[16,64,128]{2,1,0:T(8,128)S(1)} %get-tuple-element.36.wet_ref, ...), custom_call_target="tpu_custom_call" | custom-call | flops 1000000000 | bytes 1000000 | tf_op jit(solution)/shard_map/middle_rows/pallas_call | solution.py:465
  11.6 0.0 collective-permute-done.pa_ref
  11.6 0.0 collective-permute-done.1.pb_ref
  11.6 0.2 %between.1 = (f32[4,80,128]{2,1,0:T(8,128)S(1)}, f32[64,128]{1,0:T(8,128)S(1)}, f32[32,128]{1,0:T(8,128)S(1)}, f32[80,128]{1,0:T(8,128)S(1)}, f32[80,128]{1,0:T(8,128)S(1)}, /*index=5*/f32[96,128]{1,0:T(8,128)S(1)}) custom-call(f32[88,128]{1,0:T(8,128)S(1)} %collective-permute-done.pa_ref, f32[88,128]{1,0:T(8,128)S(1)} %collective-permute-done.1.pb_ref, ...), custom_call_target="tpu_custom_call" | custom-call | flops 10000000 | bytes 1000000 | tf_op jit(solution)/shard_map/between/pallas_call | solution.py:468
  11.8 2.9 %collective-permute-start.3 = (f32[96,128]{1,0:T(8,128)S(1)}, f32[96,128]{1,0:T(8,128)S(1)}, u32[]{:S(2)}, u32[]{:S(2)}) collective-permute-start(f32[96,128]{1,0:T(8,128)S(1)} %get-tuple-element.46.qb_ref), channel_id=1, source_target_pairs={{0,248},{1,249},{2,250},{3,251},{4,252},{5,253},{6,254},{7,255},{8... | collective-permute-start | bytes 147464 | tf_op jit(solution)/shard_map/ppermute | solution.py:443
  14.8 3.0 %collective-permute-start.2 = (f32[80,128]{1,0:T(8,128)S(1)}, f32[80,128]{1,0:T(8,128)S(1)}, u32[]{:S(2)}, u32[]{:S(2)}) collective-permute-start(f32[80,128]{1,0:T(8,128)S(1)} %get-tuple-element.45.qa_ref), channel_id=1, source_target_pairs={{0,8},{1,9},{2,10},{3,11},{4,12},{5,13},{6,14},{7,15},{8,0},{9,1},... | collective-permute-start | bytes 122888 | tf_op jit(solution)/shard_map/ppermute | solution.py:443
  17.8 1.9 %outer_rows.1.g2_ref = f32[512,128]{1,0:T(8,128)S(1)} custom-call(f32[1024,128]{1,0:T(8,128)S(1)} %get-tuple-element.30.fk_ref, f32[64,128]{1,0:T(8,128)S(1)} %get-tuple-element.52.fb_ref, bf16[128,144]{1,0:T(8,128)(2,1)S(1)} %get-tuple-element.37.w1_ref, bf16[512,128]{1,0:T(8,128)(2,1)S(1)} %get-tuple-element.38.w2_ref, ...), custom_call_target="tpu_custom_call" | custom-call | flops 500000000 | bytes 1000000 | tf_op jit(solution)/shard_map/outer_rows/pallas_call | solution.py:475
  19.7 0.0 collective-permute-done.2.ha_ref
  19.7 0.0 collective-permute-done.3.hb_ref
  19.7 2.4 %closing.1 = (f32[16,64,128]{2,1,0:T(8,128)}, f32[64,128]{1,0:T(8,128)}, f32[64,128]{1,0:T(8,128)}) custom-call(f32[80,128]{1,0:T(8,128)S(1)} %get-tuple-element.45.qa_ref, f32[96,128]{1,0:T(8,128)S(1)} %get-tuple-element.46.qb_ref, f32[80,128]{1,0:T(8,128)S(1)} %collective-permute-done.2.ha_ref, f32[96,128]{1,0:T(8,128)S(1)} %collective-permute-done.3.hb_ref, ...), custom_call_target="tpu_custom_call" | custom-call | flops 100000000 | bytes 3000000 | tf_op jit(solution)/shard_map/closing/pallas_call | solution.py:477
Async XLA Ops:
  0.6 3.5 %copy-start.1 = (bf16[512,128]{1,0:T(8,128)(2,1)S(1)}, bf16[512,128]{1,0:T(8,128)(2,1)}, u32[]{:S(2)}) copy-start(bf16[512,128]{1,0:T(8,128)(2,1)} %w2_ref.1) | copy-start | bytes 393220
  0.6 3.5 %copy-start = (bf16[9,128,16]{1,2,0:T(8,128)(2,1)S(1)}, bf16[9,128,16]{1,2,0:T(8,128)(2,1)}, u32[]{:S(2)}) copy-start(bf16[9,128,16]{1,2,0:T(8,128)(2,1)} %param.15) | copy-start | bytes 110596
  0.7 3.5 %copy-start.2 = (bf16[16,512]{1,0:T(8,128)(2,1)S(1)}, bf16[16,512]{1,0:T(8,128)(2,1)}, u32[]{:S(2)}) copy-start(bf16[16,512]{1,0:T(8,128)(2,1)} %w3_ref.1) | copy-start | bytes 49156
  2.7 8.8 %collective-permute-start = (f32[88,128]{1,0:T(8,128)S(1)}, f32[88,128]{1,0:T(8,128)S(1)}, u32[]{:S(2)}, u32[]{:S(2)}) collective-permute-start(f32[88,128]{1,0:T(8,128)S(1)} %get-tuple-element.28), channel_id=1, source_target_pairs={{0,1},{1,0},{2,3},{3,2},{4,5},{5,4},{6,7},{7,6},{8,9},{9,8},{10,11... | collective-permute-start | bytes 135176 | tf_op jit(solution)/shard_map/ppermute | solution.py:443
  4.2 7.4 %collective-permute-start.1 = (f32[88,128]{1,0:T(8,128)S(1)}, f32[88,128]{1,0:T(8,128)S(1)}, u32[]{:S(2)}, u32[]{:S(2)}) collective-permute-start(f32[88,128]{1,0:T(8,128)S(1)} %get-tuple-element.32), channel_id=1, source_target_pairs={{0,8},{1,2},{2,1},{3,4},{4,3},{5,6},{6,5},{7,255},{8,0},{9,10},{10... | collective-permute-start | bytes 135176 | tf_op jit(solution)/shard_map/ppermute | solution.py:443
  11.8 7.9 %collective-permute-start.3 = (f32[96,128]{1,0:T(8,128)S(1)}, f32[96,128]{1,0:T(8,128)S(1)}, u32[]{:S(2)}, u32[]{:S(2)}) collective-permute-start(f32[96,128]{1,0:T(8,128)S(1)} %get-tuple-element.46.qb_ref), channel_id=1, source_target_pairs={{0,248},{1,249},{2,250},{3,251},{4,252},{5,253},{6,254},{7,255},{8... | collective-permute-start | bytes 147464 | tf_op jit(solution)/shard_map/ppermute | solution.py:443
  14.8 4.9 %collective-permute-start.2 = (f32[80,128]{1,0:T(8,128)S(1)}, f32[80,128]{1,0:T(8,128)S(1)}, u32[]{:S(2)}, u32[]{:S(2)}) collective-permute-start(f32[80,128]{1,0:T(8,128)S(1)} %get-tuple-element.45.qa_ref), channel_id=1, source_target_pairs={{0,8},{1,9},{2,10},{3,11},{4,12},{5,13},{6,14},{7,15},{8,0},{9,1},... | collective-permute-start | bytes 122888 | tf_op jit(solution)/shard_map/ppermute | solution.py:443

commit v5 on v4

--- a/solution.py
+++ b/solution.py
@@ -114,11 +114,12 @@
         own = jnp.concatenate([t_ref[:, r, :], wet_ref[:, r, :]], axis=0)
         feature = fk_ref[16 * r : 16 * r + 16, :]
         rows = [x[first : first + 8] for x in (forcing, column, np_ref[0], np_ref[1])]
-        return own, jnp.concatenate([own, feature] + rows + [edge_pairs(t_ref, wet_ref, first)], axis=0)
+        pairs = edge_pairs(t_ref, wet_ref, first)
+        return jnp.concatenate([own, pairs], axis=0), jnp.concatenate([own, feature] + rows + [pairs], axis=0)
 
     own_low, low = payload(0, 0)
     own_high, high = payload(63, 56)
-    own_ref[...] = jnp.concatenate([own_low, own_high], axis=0)
+    own_ref[...] = jnp.concatenate([own_low[0:32], own_high[0:32], own_low[32:40], own_high[32:40]], axis=0)
     even = lat % 2 == 0
     pa_ref[...] = jnp.where(even, high, low)
     pb_ref[...] = jnp.where(even, low, high)
@@ -267,7 +268,7 @@
     pl.when(early_rows())(functools.partial(inner_chunk, fk_ref, weights, planes, 0, g_ref, 0))
 
 
-def middle_rows(fk_ref, t_ref, wet_ref, w1_ref, w2_ref, w3_ref, done_ref, g_ref, rt_ref, rf_ref, *planes):
+def middle_rows(fk_ref, t_ref, wet_ref, own_ref, w1_ref, w2_ref, w3_ref, done_ref, g_ref, rt_ref, rf_ref, *planes):
     weights = (w1_ref, w2_ref, w3_ref)
     early = early_rows()
     pl.when(jnp.logical_not(early))(functools.partial(inner_chunk, fk_ref, weights, planes, 0, g_ref, 0))
@@ -277,8 +278,11 @@
         g_ref[0:256, :] = done_ref[...]
 
     pl.when(jnp.logical_not(late_rows()))(functools.partial(inner_chunk, fk_ref, weights, planes, 1, g_ref, 16))
+    rt_ref[0:8, :] = own_ref[64:72, :]
+    rt_ref[56:64, :] = own_ref[72:80, :]
     for i in range(0, 64, 8):
-        rt_ref[i : i + 8, :] = edge_pairs(t_ref, wet_ref, i)
+        if 0 < i < 56:
+            rt_ref[i : i + 8, :] = edge_pairs(t_ref, wet_ref, i)
         rf_ref[i : i + 8, :] = edge_features(fk_ref, i)
     inner_chunk(fk_ref, weights, planes, 2, g_ref, 32)
 
@@ -449,7 +453,7 @@
     tv, warm, wet, fk, fc, own, both, mx, pa, pb = call(
         inside,
         (shape(*cube), shape(*cube), shape(*cube), shape(1024, 128), shape(2, 64, 128),
-         shape(*flat), shape(2, 64, 128), shape(24, 128), shape(88, 128), shape(88, 128)),
+         shape(*tall), shape(2, 64, 128), shape(24, 128), shape(88, 128), shape(88, 128)),
         scratch=(pltpu.VMEM(cube, jnp.int32), pltpu.VMEM(flat, jnp.int32), pltpu.SMEM((16,), F32),
                  pltpu.VMEM((16, 80, 128), F32), pltpu.SemaphoreType.DMA((12,))),
         specs=[HB] * 6, name="inside", flops=10**7, moved=2 * 10**6,
@@ -463,8 +467,8 @@
     pb, gp = lax.optimization_barrier((pb, gp))
     rb = swap(pb, LAT_B)
     g1, rt, rf = call(middle_rows, (shape(*inner), shape(*flat), shape(*flat)), scratch=planes,
-                      specs=[VM] * 7, name="middle_rows", flops=10**9, moved=10**6,
-                      )(fk, tv, wet, v1, v2, v3, gp)
+                      specs=[VM] * 8, name="middle_rows", flops=10**9, moved=10**6,
+                      )(fk, tv, wet, own, v1, v2, v3, gp)
     e4, fb, dd, rfx, qa, qb = call(
         between,
         (shape(4, 80, 128), shape(64, 128), shape(32, 128), shape(*tall), shape(*tall), shape(96, 128)),

time: 22.4 us -> 22.4 us (level)
  transfers between devices with their start and end apart: 4 -> 4, of which waited for: 0 -> 0; matrix products, arithmetic and copies ran while one was open for 0% -> 0% of each run, Pallas kernels for 33% -> 34%
where the time goes in v5:
time: 22.4 us; the launch traced here: 22.3 us
  Pallas kernels  12.3 us (55%)
  starting transfers between devices  9.17 us (41%)
  between operations  0.88 us (4%)
    ppermute x4, starting transfers between devices, swap(): return lax.ppermute(x, ('lon', 'lat'), pairs)  9.17 us
    pallas_call x1, Pallas kernels, on_device(): call(middle_rows, (shape(*inner), shape(*flat), shape(*flat)), scratch=pl...  5.48 us
    pallas_call x1, Pallas kernels, on_device(): call(closing, (shape(*cube), shape(*flat), shape(*flat)), scratch=(pltpu....  2.43 us
    pallas_call x1, Pallas kernels, on_device(): call(inside, (shape(*cube), shape(*cube), shape(*cube), shape(1024, 128),...  2.07 us
    pallas_call x1, Pallas kernels, on_device(): call(outer_rows, shape(512, 128), scratch=planes, specs=[VM] * 6, name='o...  1.96 us
  transfers between devices with their start and end apart: 4, of which 0 were waited for; matrix products, arithmetic and copies ran while one was open for 0% of the time, Pallas kernels for 34%

profile of v5, /device:TPU:5, one launch (start us, length us, event | category | flops | bytes accessed | tf_op | source)
XLA Modules:
  0.0 22.3 jit_solution(10044076081921262968)
XLA Ops:
  0.6 0.0 copy-start.1
  0.6 0.0 copy-start
  0.7 0.0 copy-start.2
  0.7 2.1 %inside.1 = (f32[16,64,128]{2,1,0:T(8,128)S(1)}, f32[16,64,128]{2,1,0:T(8,128)S(1)}, f32[16,64,128]{2,1,0:T(8,128)S(1)}, f32[1024,128]{1,0:T(8,128)S(1)}, f32[2,...) custom-call(f32[16,64,128]{2,1,0:T(8,128)} %t_hbm.1, ...), custom_call_target="tpu_custom_call" | custom-call | flops 10000000 | bytes 2000000 | tf_op jit(solution)/shard_map/inside/pallas_call | solution.py:453
  2.7 1.4 %collective-permute-start = (f32[88,128]{1,0:T(8,128)S(1)}, f32[88,128]{1,0:T(8,128)S(1)}, u32[]{:S(2)}, u32[]{:S(2)}) collective-permute-start(f32[88,128]{1,0:T(8,128)S(1)} %get-tuple-element.28), channel_id=1, source_target_pairs={{0,1},{1,0},{2,3},{3,2},{4,5},{5,4},{6,7},{7,6},{8,9},{9,8},{10,11... | collective-permute-start | bytes 135176 | tf_op jit(solution)/shard_map/ppermute | solution.py:447
  4.1 0.0 copy-done.1
  4.1 0.0 copy-done
  4.1 0.0 copy-done.2
  4.1 0.1 ahead.1
  4.2 1.9 %collective-permute-start.1 = (f32[88,128]{1,0:T(8,128)S(1)}, f32[88,128]{1,0:T(8,128)S(1)}, u32[]{:S(2)}, u32[]{:S(2)}) collective-permute-start(f32[88,128]{1,0:T(8,128)S(1)} %get-tuple-element.32), channel_id=1, source_target_pairs={{0,8},{1,2},{2,1},{3,4},{4,3},{5,6},{6,5},{7,255},{8,0},{9,10},{10... | collective-permute-start | bytes 135176 | tf_op jit(solution)/shard_map/ppermute | solution.py:447
  6.2 5.5 %middle_rows.1 = (f32[768,128]{1,0:T(8,128)S(1)}, f32[64,128]{1,0:T(8,128)S(1)}, f32[64,128]{1,0:T(8,128)S(1)}) custom-call(f32[1024,128]{1,0:T(8,128)S(1)} %get-tuple-element.30.fk_ref, f32[16,64,128]{2,1,0:T(8,128)S(1)} %get-tuple-element.35.t_ref, f32[16,64,128]{2,1,0:T(8,128)S(1)} %get-tuple-element.36.wet_ref, f32[80,128]{1,0:T(8,128)S(1)} %get-tuple-element.33.own_ref, ...), custom_call_target="tpu_custom_call" | custom-call | flops 1000000000 | bytes 1000000 | tf_op jit(solution)/shard_map/middle_rows/pallas_call | solution.py:469
  11.6 0.0 collective-permute-done.pa_ref
  11.7 0.0 collective-permute-done.1.pb_ref
  11.7 0.2 %between.1 = (f32[4,80,128]{2,1,0:T(8,128)S(1)}, f32[64,128]{1,0:T(8,128)S(1)}, f32[32,128]{1,0:T(8,128)S(1)}, f32[80,128]{1,0:T(8,128)S(1)}, f32[80,128]{1,0:T(8,128)S(1)}, /*index=5*/f32[96,128]{1,0:T(8,128)S(1)}) custom-call(f32[88,128]{1,0:T(8,128)S(1)} %collective-permute-done.pa_ref, f32[88,128]{1,0:T(8,128)S(1)} %collective-permute-done.1.pb_ref, ...), custom_call_target="tpu_custom_call" | custom-call | flops 10000000 | bytes 1000000 | tf_op jit(solution)/shard_map/between/pallas_call | solution.py:472
  11.9 2.9 %collective-permute-start.3 = (f32[96,128]{1,0:T(8,128)S(1)}, f32[96,128]{1,0:T(8,128)S(1)}, u32[]{:S(2)}, u32[]{:S(2)}) collective-permute-start(f32[96,128]{1,0:T(8,128)S(1)} %get-tuple-element.46.qb_ref), channel_id=1, source_target_pairs={{0,248},{1,249},{2,250},{3,251},{4,252},{5,253},{6,254},{7,255},{8... | collective-permute-start | bytes 147464 | tf_op jit(solution)/shard_map/ppermute | solution.py:447
  14.8 3.0 %collective-permute-start.2 = (f32[80,128]{1,0:T(8,128)S(1)}, f32[80,128]{1,0:T(8,128)S(1)}, u32[]{:S(2)}, u32[]{:S(2)}) collective-permute-start(f32[80,128]{1,0:T(8,128)S(1)} %get-tuple-element.45.qa_ref), channel_id=1, source_target_pairs={{0,8},{1,9},{2,10},{3,11},{4,12},{5,13},{6,14},{7,15},{8,0},{9,1},... | collective-permute-start | bytes 122888 | tf_op jit(solution)/shard_map/ppermute | solution.py:447
  17.8 2.0 %outer_rows.1.g2_ref = f32[512,128]{1,0:T(8,128)S(1)} custom-call(f32[1024,128]{1,0:T(8,128)S(1)} %get-tuple-element.30.fk_ref, f32[64,128]{1,0:T(8,128)S(1)} %get-tuple-element.52.fb_ref, bf16[128,144]{1,0:T(8,128)(2,1)S(1)} %get-tuple-element.37.w1_ref, bf16[512,128]{1,0:T(8,128)(2,1)S(1)} %get-tuple-element.38.w2_ref, ...), custom_call_target="tpu_custom_call" | custom-call | flops 500000000 | bytes 1000000 | tf_op jit(solution)/shard_map/outer_rows/pallas_call | solution.py:479
  19.7 0.0 collective-permute-done.2.ha_ref
  19.7 0.0 collective-permute-done.3.hb_ref
  19.8 2.4 %closing.1 = (f32[16,64,128]{2,1,0:T(8,128)}, f32[64,128]{1,0:T(8,128)}, f32[64,128]{1,0:T(8,128)}) custom-call(f32[80,128]{1,0:T(8,128)S(1)} %get-tuple-element.45.qa_ref, f32[96,128]{1,0:T(8,128)S(1)} %get-tuple-element.46.qb_ref, f32[80,128]{1,0:T(8,128)S(1)} %collective-permute-done.2.ha_ref, f32[96,128]{1,0:T(8,128)S(1)} %collective-permute-done.3.hb_ref, ...), custom_call_target="tpu_custom_call" | custom-call | flops 100000000 | bytes 3000000 | tf_op jit(solution)/shard_map/closing/pallas_call | solution.py:481
Async XLA Ops:
  0.6 3.5 %copy-start.1 = (bf16[512,128]{1,0:T(8,128)(2,1)S(1)}, bf16[512,128]{1,0:T(8,128)(2,1)}, u32[]{:S(2)}) copy-start(bf16[512,128]{1,0:T(8,128)(2,1)} %w2_ref.1) | copy-start | bytes 393220
  0.6 3.5 %copy-start = (bf16[9,128,16]{1,2,0:T(8,128)(2,1)S(1)}, bf16[9,128,16]{1,2,0:T(8,128)(2,1)}, u32[]{:S(2)}) copy-start(bf16[9,128,16]{1,2,0:T(8,128)(2,1)} %param.15) | copy-start | bytes 110596
  0.7 3.5 %copy-start.2 = (bf16[16,512]{1,0:T(8,128)(2,1)S(1)}, bf16[16,512]{1,0:T(8,128)(2,1)}, u32[]{:S(2)}) copy-start(bf16[16,512]{1,0:T(8,128)(2,1)} %w3_ref.1) | copy-start | bytes 49156
  2.7 8.9 %collective-permute-start = (f32[88,128]{1,0:T(8,128)S(1)}, f32[88,128]{1,0:T(8,128)S(1)}, u32[]{:S(2)}, u32[]{:S(2)}) collective-permute-start(f32[88,128]{1,0:T(8,128)S(1)} %get-tuple-element.28), channel_id=1, source_target_pairs={{0,1},{1,0},{2,3},{3,2},{4,5},{5,4},{6,7},{7,6},{8,9},{9,8},{10,11... | collective-permute-start | bytes 135176 | tf_op jit(solution)/shard_map/ppermute | solution.py:447
  4.2 7.4 %collective-permute-start.1 = (f32[88,128]{1,0:T(8,128)S(1)}, f32[88,128]{1,0:T(8,128)S(1)}, u32[]{:S(2)}, u32[]{:S(2)}) collective-permute-start(f32[88,128]{1,0:T(8,128)S(1)} %get-tuple-element.32), channel_id=1, source_target_pairs={{0,8},{1,2},{2,1},{3,4},{4,3},{5,6},{6,5},{7,255},{8,0},{9,10},{10... | collective-permute-start | bytes 135176 | tf_op jit(solution)/shard_map/ppermute | solution.py:447
  11.9 7.8 %collective-permute-start.3 = (f32[96,128]{1,0:T(8,128)S(1)}, f32[96,128]{1,0:T(8,128)S(1)}, u32[]{:S(2)}, u32[]{:S(2)}) collective-permute-start(f32[96,128]{1,0:T(8,128)S(1)} %get-tuple-element.46.qb_ref), channel_id=1, source_target_pairs={{0,248},{1,249},{2,250},{3,251},{4,252},{5,253},{6,254},{7,255},{8... | collective-permute-start | bytes 147464 | tf_op jit(solution)/shard_map/ppermute | solution.py:447
  14.8 4.9 %collective-permute-start.2 = (f32[80,128]{1,0:T(8,128)S(1)}, f32[80,128]{1,0:T(8,128)S(1)}, u32[]{:S(2)}, u32[]{:S(2)}) collective-permute-start(f32[80,128]{1,0:T(8,128)S(1)} %get-tuple-element.45.qa_ref), channel_id=1, source_target_pairs={{0,8},{1,9},{2,10},{3,11},{4,12},{5,13},{6,14},{7,15},{8,0},{9,1},... | collective-permute-start | bytes 122888 | tf_op jit(solution)/shard_map/ppermute | solution.py:447
